TPU v7x, 128 devices: a whole 4x4x4 slice. The times are simulated.
128 devices in a mesh: ctx: 64 (over y, z_hi, x, core), kvh: 2 (over z_lo).
Axes of the slice: x: 4, y: 4, z: 4 (z_hi: 2, z_lo: 2; z = z_hi * 2 + z_lo), core: 2. Of those that a mesh axis runs over, the one named last changes fastest.
Arguments:
- queries: bfloat16 [16384, 8192], P('ctx', 'kvh'), may hold values from -180 to 180
- keys: bfloat16 [16384, 1024], P('ctx', 'kvh'), may hold values from -6 to 6
- values: bfloat16 [16384, 1024], P('ctx', 'kvh'), may hold values from -6 to 6
- fwd_out: bfloat16 [16384, 8192], P('ctx', 'kvh'), may hold values from -4 to 4
- log_sum: float32 [64, 16384], P('kvh', 'ctx'), as said below
- out_grad: bfloat16 [16384, 8192], P('ctx', 'kvh'), may hold values from -6 to 6
- seg_ids: int32 [16384], replicated, may hold values from 0 to 15, as said below
- active: int32 [128, 16], P('ctx'), may hold values from 0 to 1, as said below
Outputs:
- grad_queries: bfloat16 [16384, 8192], P('ctx', 'kvh')
- grad_keys: bfloat16 [16384, 1024], P('ctx', 'kvh')
- grad_values: bfloat16 [16384, 1024], P('ctx', 'kvh')
Inputs may be any that keep to these rules, and one draw needn't show every extreme that they name: log_sum[h, t] is the logarithm of the sum over allowed u of exp(scores[h, t, u]) for the given queries and keys. `seg_ids`: document ids never fall along the sequence; every document has 1 to 2048 tokens, and one has exactly 2048. `active`: column 0 is 1 in every row; a row has 1 to 12 ones, and the last row exactly 12.
All inputs are finite; a program needn't handle non-finite values.
Results may differ from a plain program's by a relative error of at most 0.0049.
Values may be sent and summed in bfloat16 or wider, within the bound.
A program may use at most 64 MiB of HBM per device.

v0:
```python
import jax
import jax.numpy as jnp
from jax import lax
from jax.sharding import PartitionSpec as P

D_HEAD = 128
BLK = 128
WINBLK = 16


LOWEST = -1e30


def shifted(value, axis, steps):
    count = lax.axis_size(axis)
    first, last = (max(0, -steps), min(count, count - steps))
    return lax.ppermute(value, axis, [(source, source + steps) for source in range(first, last)])


def passed_along(value, axis, steps):
    count = lax.axis_size(axis)
    pairs = [(source, (source + steps) % count) for source in range(count)]
    return lax.ppermute(value, axis, pairs)


def body(queries, keys, values, fwd_out, log_sum, out_grad, seg_ids, active):
    device = lax.axis_index("ctx")
    tokens_here = queries.shape[0]
    kv_heads = keys.shape[1] // D_HEAD
    per_group = queries.shape[1] // D_HEAD // kv_heads
    blocks = tokens_here // BLK
    travel = WINBLK // blocks
    factor = D_HEAD ** (-0.5)
    own_first = device * tokens_here
    within = jnp.arange(BLK, dtype=jnp.int32)
    query_heads = queries.reshape(tokens_here, kv_heads, per_group, D_HEAD)
    grad_heads = out_grad.reshape(tokens_here, kv_heads, per_group, D_HEAD)
    delta_row = jnp.einsum(
        "tgjd,tgjd->gjt",
        grad_heads,
        fwd_out.reshape(tokens_here, kv_heads, per_group, D_HEAD),
        preferred_element_type=jnp.float32,
    )
    log_rows = log_sum.reshape(kv_heads, per_group, tokens_here)

    def pair_setup(turn_index, pair_index):
        query_part = pair_index // blocks
        key_part = pair_index % blocks
        source = device - turn_index
        distance = turn_index * blocks + query_part - key_part
        inside = (source >= 0) & (distance >= 0) & (distance < WINBLK)
        flag_value = active[query_part, jnp.clip(distance, 0, WINBLK - 1)]
        query_first = own_first + query_part * BLK
        key_first = source * tokens_here + key_part * BLK
        query_seg = lax.dynamic_slice_in_dim(seg_ids, query_first, BLK, 0)
        key_seg = lax.dynamic_slice_in_dim(seg_ids, jnp.maximum(key_first, 0), BLK, 0)
        allowed = ((key_first + within)[None, :] <= (query_first + within)[:, None]) & (
            key_seg[None, :] == query_seg[:, None]
        )
        return (query_part, key_part, inside & (flag_value > 0), allowed)

    def grad_update(turn_index, key_all, value_all, grad_sums):
        key_heads = key_all.reshape(tokens_here, kv_heads, D_HEAD)
        value_heads = value_all.reshape(tokens_here, kv_heads, D_HEAD)

        def one_pair(pair_index, sums_now):
            query_part, key_part, usable, allowed = pair_setup(turn_index, pair_index)

            def compute(sums_in):
                query_sum, key_sum, value_sum = sums_in
                query_rows = query_part * BLK
                key_rows = key_part * BLK
                query_block = lax.dynamic_slice_in_dim(query_heads, query_rows, BLK, 0)
                grad_block = lax.dynamic_slice_in_dim(grad_heads, query_rows, BLK, 0)
                key_block = lax.dynamic_slice_in_dim(key_heads, key_rows, BLK, 0)
                value_block = lax.dynamic_slice_in_dim(value_heads, key_rows, BLK, 0)
                scores = (
                    jnp.einsum(
                        "tgjd,ugd->gjtu", query_block, key_block, preferred_element_type=jnp.float32
                    )
                    * factor
                )
                log_part = lax.dynamic_slice_in_dim(log_rows, query_rows, BLK, 2)
                delta_part = lax.dynamic_slice_in_dim(delta_row, query_rows, BLK, 2)
                weights = jnp.exp(jnp.where(allowed, scores - log_part[..., None], LOWEST))
                weights_half = weights.astype(jnp.bfloat16)
                grad_weights = jnp.einsum(
                    "tgjd,ugd->gjtu", grad_block, value_block, preferred_element_type=jnp.float32
                )
                grad_scores = (weights * (grad_weights - delta_part[..., None])).astype(
                    jnp.bfloat16
                )
                query_term = (
                    jnp.einsum(
                        "gjtu,ugd->tgjd", grad_scores, key_block, preferred_element_type=jnp.float32
                    )
                    * factor
                ).reshape(BLK, -1)
                key_term = (
                    jnp.einsum(
                        "gjtu,tgjd->ugd",
                        grad_scores,
                        query_block,
                        preferred_element_type=jnp.float32,
                    )
                    * factor
                ).reshape(BLK, -1)
                value_term = jnp.einsum(
                    "gjtu,tgjd->ugd", weights_half, grad_block, preferred_element_type=jnp.float32
                ).reshape(BLK, -1)
                query_sum = lax.dynamic_update_slice_in_dim(
                    query_sum,
                    lax.dynamic_slice_in_dim(query_sum, query_rows, BLK, 0) + query_term,
                    query_rows,
                    0,
                )
                key_sum = lax.dynamic_update_slice_in_dim(
                    key_sum,
                    lax.dynamic_slice_in_dim(key_sum, key_rows, BLK, 0) + key_term,
                    key_rows,
                    0,
                )
                value_sum = lax.dynamic_update_slice_in_dim(
                    value_sum,
                    lax.dynamic_slice_in_dim(value_sum, key_rows, BLK, 0) + value_term,
                    key_rows,
                    0,
                )
                return (query_sum, key_sum, value_sum)

            return lax.cond(usable, compute, lambda sums_in: sums_in, sums_now)

        return lax.fori_loop(0, blocks * blocks, one_pair, grad_sums)

    empty_keys = jnp.zeros(keys.shape, jnp.float32)
    empty_query = jnp.zeros(queries.shape, jnp.float32)
    part_banks = ()

    def turn_compute(turn_index, loop_state):
        pair_now, query_sum, key_sums, part_now = loop_state
        key_all = pair_now[0]
        value_all = pair_now[1]
        query_sum, key_sum, value_sum = grad_update(
            turn_index, key_all, value_all, (query_sum, key_sums[0], key_sums[1])
        )
        key_sums = (key_sum, value_sum)
        return (pair_now, query_sum, key_sums, part_now)

    def one_turn(turn_index, loop_state):
        pair_now, query_sum, key_sums, part_now = turn_compute(turn_index, loop_state)
        pair_now = shifted((pair_now[0], pair_now[1]), "ctx", 1)
        key_sums = passed_along((key_sums[0], key_sums[1]), "ctx", 1)
        return (pair_now, query_sum, key_sums, part_now)

    loop_state = ((keys, values), empty_query, (empty_keys, empty_keys), part_banks)
    loop_state = lax.fori_loop(0, travel, one_turn, loop_state)
    pair_now, query_sum, key_sums, part_now = turn_compute(travel, loop_state)
    key_sum, value_sum = (
        passed_along(key_sums[0].astype(jnp.bfloat16), "ctx", -travel).astype(jnp.float32),
        passed_along(key_sums[1].astype(jnp.bfloat16), "ctx", -travel).astype(jnp.float32),
    )
    return (
        query_sum.astype(jnp.bfloat16),
        key_sum.astype(jnp.bfloat16),
        value_sum.astype(jnp.bfloat16),
    )


def solution(mesh):
    placed = (
        P("ctx", "kvh"),
        P("ctx", "kvh"),
        P("ctx", "kvh"),
        P("ctx", "kvh"),
        P("kvh", "ctx"),
        P("ctx", "kvh"),
        P(),
        P("ctx", None),
    )
    return jax.shard_map(
        body,
        mesh=mesh,
        in_specs=placed,
        out_specs=(P("ctx", "kvh"), P("ctx", "kvh"), P("ctx", "kvh")),
        check_vma=False,
    )
```

profile of v0, /device:TPU:1, one launch (start us, length us, event | category | flops | bytes accessed | tf_op | source)
XLA Modules:
  0.0 551.5 jit_solution(18178509999186016245)
XLA Ops:
  33.7 413.6 %while.96 = (s32[]{:T(128)}, bf16[256,512]{0,1:T(8,128)(2,1)S(1)}, bf16[256,512]{0,1:T(8,128)(2,1)}, f32[256,4096]{0,1:T(8,128)}, f32[256,512]{0,1:T(8,128)S(1)}...) while((s32[]{:T(128)}, bf16[256,512]{0,1:T(8,128)(2,1)S(1)}, ...), condition=%wide.region_5.6_spmd.clone.clone, body=%wide.region_0.5_spmd.clone.clone.sunk | while | flops 676053248 | bytes 44572712 | solution.py:156
  39.0 34.7 %while.98 = (s32[]{:T(128)}, f32[256,4096]{0,1:T(8,128)}, f32[256,512]{0,1:T(8,128)S(1)}, f32[256,512]{0,1:T(8,128)S(1)}, s32[]{:T(128)}, /*index=5*/pred[]{:T(5...) while((s32[]{:T(128)}, f32[256,4096]{0,1:T(8,128)}, ...), condition=%wide.region_4.4_spmd.clone, body=%wide.region_1.3_spmd.clone.sunk | while | flops 676053248 | bytes 34085800 | solution.py:133
  40.3 9.8 %conditional.8 = ((f32[256,4096]{0,1:T(8,128)}, f32[256,512]{0,1:T(8,128)S(1)}, f32[256,512]{0,1:T(8,128)S(1)})) conditional(s32[]{:T(128)} %convert_element_type.71, (f32[256,4096]{0,1:T(8,128)}, f32[256,512]{0,1:T(8,128)S(1)}, f32[256,512]{0,1:T(8,128)S(1)}) %tuple.182, (s32[]{:T(128)}, f32[256,4096]{0,1:T(8,128)}, s32[]{:T(128)}, ...), branch_computations={%region_2.1_spmd, %region_3.2_spmd} | conditional | flops 676053248 | bytes 34085176 | solution.py:131
  52.8 9.7 %conditional.8 = ((f32[256,4096]{0,1:T(8,128)}, f32[256,512]{0,1:T(8,128)S(1)}, f32[256,512]{0,1:T(8,128)S(1)})) conditional(s32[]{:T(128)} %convert_element_type.71, (f32[256,4096]{0,1:T(8,128)}, f32[256,512]{0,1:T(8,128)S(1)}, f32[256,512]{0,1:T(8,128)S(1)}) %tuple.182, (s32[]{:T(128)}, f32[256,4096]{0,1:T(8,128)}, s32[]{:T(128)}, ...), branch_computations={%region_2.1_spmd, %region_3.2_spmd} | conditional | flops 676053248 | bytes 34085176 | solution.py:131
  63.9 9.7 %conditional.8 = ((f32[256,4096]{0,1:T(8,128)}, f32[256,512]{0,1:T(8,128)S(1)}, f32[256,512]{0,1:T(8,128)S(1)})) conditional(s32[]{:T(128)} %convert_element_type.71, (f32[256,4096]{0,1:T(8,128)}, f32[256,512]{0,1:T(8,128)S(1)}, f32[256,512]{0,1:T(8,128)S(1)}) %tuple.182, (s32[]{:T(128)}, f32[256,4096]{0,1:T(8,128)}, s32[]{:T(128)}, ...), branch_computations={%region_2.1_spmd, %region_3.2_spmd} | conditional | flops 676053248 | bytes 34085176 | solution.py:131
  99.0 25.0 %while.98 = (s32[]{:T(128)}, f32[256,4096]{0,1:T(8,128)}, f32[256,512]{0,1:T(8,128)S(1)}, f32[256,512]{0,1:T(8,128)S(1)}, s32[]{:T(128)}, /*index=5*/pred[]{:T(5...) while((s32[]{:T(128)}, f32[256,4096]{0,1:T(8,128)}, ...), condition=%wide.region_4.4_spmd.clone, body=%wide.region_1.3_spmd.clone.sunk | while | flops 676053248 | bytes 34085800 | solution.py:133
  100.3 9.8 %conditional.8 = ((f32[256,4096]{0,1:T(8,128)}, f32[256,512]{0,1:T(8,128)S(1)}, f32[256,512]{0,1:T(8,128)S(1)})) conditional(s32[]{:T(128)} %convert_element_type.71, (f32[256,4096]{0,1:T(8,128)}, f32[256,512]{0,1:T(8,128)S(1)}, f32[256,512]{0,1:T(8,128)S(1)}) %tuple.182, (s32[]{:T(128)}, f32[256,4096]{0,1:T(8,128)}, s32[]{:T(128)}, ...), branch_computations={%region_2.1_spmd, %region_3.2_spmd} | conditional | flops 676053248 | bytes 34085176 | solution.py:131
  114.2 9.7 %conditional.8 = ((f32[256,4096]{0,1:T(8,128)}, f32[256,512]{0,1:T(8,128)S(1)}, f32[256,512]{0,1:T(8,128)S(1)})) conditional(s32[]{:T(128)} %convert_element_type.71, (f32[256,4096]{0,1:T(8,128)}, f32[256,512]{0,1:T(8,128)S(1)}, f32[256,512]{0,1:T(8,128)S(1)}) %tuple.182, (s32[]{:T(128)}, f32[256,4096]{0,1:T(8,128)}, s32[]{:T(128)}, ...), branch_computations={%region_2.1_spmd, %region_3.2_spmd} | conditional | flops 676053248 | bytes 34085176 | solution.py:131
  149.2 5.6 %while.98 = (s32[]{:T(128)}, f32[256,4096]{0,1:T(8,128)}, f32[256,512]{0,1:T(8,128)S(1)}, f32[256,512]{0,1:T(8,128)S(1)}, s32[]{:T(128)}, /*index=5*/pred[]{:T(5...) while((s32[]{:T(128)}, f32[256,4096]{0,1:T(8,128)}, ...), condition=%wide.region_4.4_spmd.clone, body=%wide.region_1.3_spmd.clone.sunk | while | flops 676053248 | bytes 34085800 | solution.py:133
  154.8 21.9 %collective-permute-start.3 = (f32[256,512]{0,1:T(8,128)S(1)}, f32[256,512]{0,1:T(8,128)}, u32[]{:S(2)}, u32[]{:S(2)}) collective-permute-start(f32[256,512]{0,1:T(8,128)S(1)} %get-tuple-element.2277), channel_id=1, source_target_pairs={{0,2},{2,4},{4,6},{6,8},{8,10},{10,12},{12,14},{14,16},{16,18},{18... | collective-permute-start | bytes 1572872 | tf_op jit(solution)/shard_map/while/body/eval_jaxpr/ppermute | solution.py:23
  199.4 5.6 %while.98 = (s32[]{:T(128)}, f32[256,4096]{0,1:T(8,128)}, f32[256,512]{0,1:T(8,128)S(1)}, f32[256,512]{0,1:T(8,128)S(1)}, s32[]{:T(128)}, /*index=5*/pred[]{:T(5...) while((s32[]{:T(128)}, f32[256,4096]{0,1:T(8,128)}, ...), condition=%wide.region_4.4_spmd.clone, body=%wide.region_1.3_spmd.clone.sunk | while | flops 676053248 | bytes 34085800 | solution.py:133
  207.6 13.4 %collective-permute-start.2 = (f32[256,512]{0,1:T(8,128)S(1)}, f32[256,512]{0,1:T(8,128)}, u32[]{:S(2)}, u32[]{:S(2)}) collective-permute-start(f32[256,512]{0,1:T(8,128)S(1)} %get-tuple-element.2276), channel_id=1, source_target_pairs={{0,2},{2,4},{4,6},{6,8},{8,10},{10,12},{12,14},{14,16},{16,18},{18... | collective-permute-start | bytes 1572872 | tf_op jit(solution)/shard_map/while/body/eval_jaxpr/ppermute | solution.py:23
  238.1 5.6 %while.98 = (s32[]{:T(128)}, f32[256,4096]{0,1:T(8,128)}, f32[256,512]{0,1:T(8,128)S(1)}, f32[256,512]{0,1:T(8,128)S(1)}, s32[]{:T(128)}, /*index=5*/pred[]{:T(5...) while((s32[]{:T(128)}, f32[256,4096]{0,1:T(8,128)}, ...), condition=%wide.region_4.4_spmd.clone, body=%wide.region_1.3_spmd.clone.sunk | while | flops 676053248 | bytes 34085800 | solution.py:133
  243.7 8.1 %collective-permute-start.3 = (f32[256,512]{0,1:T(8,128)S(1)}, f32[256,512]{0,1:T(8,128)}, u32[]{:S(2)}, u32[]{:S(2)}) collective-permute-start(f32[256,512]{0,1:T(8,128)S(1)} %get-tuple-element.2277), channel_id=1, source_target_pairs={{0,2},{2,4},{4,6},{6,8},{8,10},{10,12},{12,14},{14,16},{16,18},{18... | collective-permute-start | bytes 1572872 | tf_op jit(solution)/shard_map/while/body/eval_jaxpr/ppermute | solution.py:23
  251.8 13.6 %collective-permute-start.2 = (f32[256,512]{0,1:T(8,128)S(1)}, f32[256,512]{0,1:T(8,128)}, u32[]{:S(2)}, u32[]{:S(2)}) collective-permute-start(f32[256,512]{0,1:T(8,128)S(1)} %get-tuple-element.2276), channel_id=1, source_target_pairs={{0,2},{2,4},{4,6},{6,8},{8,10},{10,12},{12,14},{14,16},{16,18},{18... | collective-permute-start | bytes 1572872 | tf_op jit(solution)/shard_map/while/body/eval_jaxpr/ppermute | solution.py:23
  265.4 25.8 %collective-permute-start = (bf16[256,512]{0,1:T(8,128)(2,1)}, bf16[256,512]{0,1:T(8,128)(2,1)S(1)}, u32[]{:S(2)}, u32[]{:S(2)}) collective-permute-start(bf16[256,512]{0,1:T(8,128)(2,1)} %copy.127), channel_id=1, source_target_pairs={{0,2},{2,4},{4,6},{6,8},{8,10},{10,12},{12,14},{14,16},{16,18},{18... | collective-permute-start | bytes 786440 | tf_op jit(solution)/shard_map/while/body/eval_jaxpr/ppermute | solution.py:17
  291.2 6.5 %collective-permute-start.1 = (bf16[256,512]{0,1:T(8,128)(2,1)}, bf16[256,512]{0,1:T(8,128)(2,1)}, u32[]{:S(2)}, u32[]{:S(2)}) collective-permute-start(bf16[256,512]{0,1:T(8,128)(2,1)} %copy.128), channel_id=1, source_target_pairs={{0,2},{2,4},{4,6},{6,8},{8,10},{10,12},{12,14},{14,16},{16,18},{18... | collective-permute-start | bytes 786440 | tf_op jit(solution)/shard_map/while/body/eval_jaxpr/ppermute | solution.py:17
  306.6 5.6 %while.98 = (s32[]{:T(128)}, f32[256,4096]{0,1:T(8,128)}, f32[256,512]{0,1:T(8,128)S(1)}, f32[256,512]{0,1:T(8,128)S(1)}, s32[]{:T(128)}, /*index=5*/pred[]{:T(5...) while((s32[]{:T(128)}, f32[256,4096]{0,1:T(8,128)}, ...), condition=%wide.region_4.4_spmd.clone, body=%wide.region_1.3_spmd.clone.sunk | while | flops 676053248 | bytes 34085800 | solution.py:133
  312.2 9.2 %collective-permute-start.3 = (f32[256,512]{0,1:T(8,128)S(1)}, f32[256,512]{0,1:T(8,128)}, u32[]{:S(2)}, u32[]{:S(2)}) collective-permute-start(f32[256,512]{0,1:T(8,128)S(1)} %get-tuple-element.2277), channel_id=1, source_target_pairs={{0,2},{2,4},{4,6},{6,8},{8,10},{10,12},{12,14},{14,16},{16,18},{18... | collective-permute-start | bytes 1572872 | tf_op jit(solution)/shard_map/while/body/eval_jaxpr/ppermute | solution.py:23
  321.4 13.6 %collective-permute-start.2 = (f32[256,512]{0,1:T(8,128)S(1)}, f32[256,512]{0,1:T(8,128)}, u32[]{:S(2)}, u32[]{:S(2)}) collective-permute-start(f32[256,512]{0,1:T(8,128)S(1)} %get-tuple-element.2276), channel_id=1, source_target_pairs={{0,2},{2,4},{4,6},{6,8},{8,10},{10,12},{12,14},{14,16},{16,18},{18... | collective-permute-start | bytes 1572872 | tf_op jit(solution)/shard_map/while/body/eval_jaxpr/ppermute | solution.py:23
  335.0 6.5 %collective-permute-start = (bf16[256,512]{0,1:T(8,128)(2,1)}, bf16[256,512]{0,1:T(8,128)(2,1)S(1)}, u32[]{:S(2)}, u32[]{:S(2)}) collective-permute-start(bf16[256,512]{0,1:T(8,128)(2,1)} %copy.127), channel_id=1, source_target_pairs={{0,2},{2,4},{4,6},{6,8},{8,10},{10,12},{12,14},{14,16},{16,18},{18... | collective-permute-start | bytes 786440 | tf_op jit(solution)/shard_map/while/body/eval_jaxpr/ppermute | solution.py:17
  341.5 14.0 %collective-permute-start.1 = (bf16[256,512]{0,1:T(8,128)(2,1)}, bf16[256,512]{0,1:T(8,128)(2,1)}, u32[]{:S(2)}, u32[]{:S(2)}) collective-permute-start(bf16[256,512]{0,1:T(8,128)(2,1)} %copy.128), channel_id=1, source_target_pairs={{0,2},{2,4},{4,6},{6,8},{8,10},{10,12},{12,14},{14,16},{16,18},{18... | collective-permute-start | bytes 786440 | tf_op jit(solution)/shard_map/while/body/eval_jaxpr/ppermute | solution.py:17
  364.4 5.6 %while.98 = (s32[]{:T(128)}, f32[256,4096]{0,1:T(8,128)}, f32[256,512]{0,1:T(8,128)S(1)}, f32[256,512]{0,1:T(8,128)S(1)}, s32[]{:T(128)}, /*index=5*/pred[]{:T(5...) while((s32[]{:T(128)}, f32[256,4096]{0,1:T(8,128)}, ...), condition=%wide.region_4.4_spmd.clone, body=%wide.region_1.3_spmd.clone.sunk | while | flops 676053248 | bytes 34085800 | solution.py:133
  372.5 16.4 %collective-permute-start.2 = (f32[256,512]{0,1:T(8,128)S(1)}, f32[256,512]{0,1:T(8,128)}, u32[]{:S(2)}, u32[]{:S(2)}) collective-permute-start(f32[256,512]{0,1:T(8,128)S(1)} %get-tuple-element.2276), channel_id=1, source_target_pairs={{0,2},{2,4},{4,6},{6,8},{8,10},{10,12},{12,14},{14,16},{16,18},{18... | collective-permute-start | bytes 1572872 | tf_op jit(solution)/shard_map/while/body/eval_jaxpr/ppermute | solution.py:23
  388.9 6.4 %collective-permute-start = (bf16[256,512]{0,1:T(8,128)(2,1)}, bf16[256,512]{0,1:T(8,128)(2,1)S(1)}, u32[]{:S(2)}, u32[]{:S(2)}) collective-permute-start(bf16[256,512]{0,1:T(8,128)(2,1)} %copy.127), channel_id=1, source_target_pairs={{0,2},{2,4},{4,6},{6,8},{8,10},{10,12},{12,14},{14,16},{16,18},{18... | collective-permute-start | bytes 786440 | tf_op jit(solution)/shard_map/while/body/eval_jaxpr/ppermute | solution.py:17
  408.4 5.6 %while.98 = (s32[]{:T(128)}, f32[256,4096]{0,1:T(8,128)}, f32[256,512]{0,1:T(8,128)S(1)}, f32[256,512]{0,1:T(8,128)S(1)}, s32[]{:T(128)}, /*index=5*/pred[]{:T(5...) while((s32[]{:T(128)}, f32[256,4096]{0,1:T(8,128)}, ...), condition=%wide.region_4.4_spmd.clone, body=%wide.region_1.3_spmd.clone.sunk | while | flops 676053248 | bytes 34085800 | solution.py:133
  416.6 6.7 %collective-permute-start.2 = (f32[256,512]{0,1:T(8,128)S(1)}, f32[256,512]{0,1:T(8,128)}, u32[]{:S(2)}, u32[]{:S(2)}) collective-permute-start(f32[256,512]{0,1:T(8,128)S(1)} %get-tuple-element.2276), channel_id=1, source_target_pairs={{0,2},{2,4},{4,6},{6,8},{8,10},{10,12},{12,14},{14,16},{16,18},{18... | collective-permute-start | bytes 1572872 | tf_op jit(solution)/shard_map/while/body/eval_jaxpr/ppermute | solution.py:23
  423.2 16.1 %collective-permute-start = (bf16[256,512]{0,1:T(8,128)(2,1)}, bf16[256,512]{0,1:T(8,128)(2,1)S(1)}, u32[]{:S(2)}, u32[]{:S(2)}) collective-permute-start(bf16[256,512]{0,1:T(8,128)(2,1)} %copy.127), channel_id=1, source_target_pairs={{0,2},{2,4},{4,6},{6,8},{8,10},{10,12},{12,14},{14,16},{16,18},{18... | collective-permute-start | bytes 786440 | tf_op jit(solution)/shard_map/while/body/eval_jaxpr/ppermute | solution.py:17
  449.9 5.7 %while.97 = (s32[]{:T(128)}, f32[256,4096]{0,1:T(8,128)}, f32[256,512]{0,1:T(8,128)S(1)}, f32[256,512]{0,1:T(8,128)S(1)}, pred[]{:T(512)}, /*index=5*/s32[2,16]{...) while((s32[]{:T(128)}, f32[256,4096]{0,1:T(8,128)}, ...), condition=%wide.region_9.10_spmd.clone.clone, body=%wide.region_6.9_spmd.clone.clone.sunk | while | flops 676053248 | bytes 34086296 | solution.py:133
  455.8 36.7 %collective-permute-start.4 = (bf16[256,512]{1,0:T(8,128)(2,1)S(1)}, bf16[256,512]{1,0:T(8,128)(2,1)S(1)}, u32[]{:S(2)}, u32[]{:S(2)}) collective-permute-start(bf16[256,512]{1,0:T(8,128)(2,1)S(1)} %copy.51), channel_id=1, source_target_pairs={{0,112},{2,114},{4,116},{6,118},{8,120},{10,122},{12,124},{14,126}... | collective-permute-start | bytes 786440 | tf_op jit(solution)/shard_map/ppermute | solution.py:23
  492.7 7.1 %collective-permute-start.5 = (bf16[256,512]{1,0:T(8,128)(2,1)S(1)}, bf16[256,512]{1,0:T(8,128)(2,1)S(1)}, u32[]{:S(2)}, u32[]{:S(2)}) collective-permute-start(bf16[256,512]{1,0:T(8,128)(2,1)S(1)} %copy.52), channel_id=1, source_target_pairs={{0,112},{2,114},{4,116},{6,118},{8,120},{10,122},{12,124},{14,126}... | collective-permute-start | bytes 786440 | tf_op jit(solution)/shard_map/ppermute | solution.py:23
  504.4 42.8 %collective-permute-done.4 = bf16[256,512]{1,0:T(8,128)(2,1)S(1)} collective-permute-done((bf16[256,512]{1,0:T(8,128)(2,1)S(1)}, bf16[256,512]{1,0:T(8,128)(2,1)S(1)}, u32[]{:S(2)}, u32[]{:S(2)}) %collective-permute-start.4) | collective-permute-done | bytes 262176 | tf_op jit(solution)/shard_map/ppermute | solution.py:23
  (287 shorter events, 258.9 us)
Async XLA Ops:
  73.6 8.7 %collective-permute-start.3 = (f32[256,512]{0,1:T(8,128)S(1)}, f32[256,512]{0,1:T(8,128)}, u32[]{:S(2)}, u32[]{:S(2)}) collective-permute-start(f32[256,512]{0,1:T(8,128)S(1)} %get-tuple-element.2277), channel_id=1, source_target_pairs={{0,2},{2,4},{4,6},{6,8},{8,10},{10,12},{12,14},{14,16},{16,18},{18... | collective-permute-start | bytes 1572872 | tf_op jit(solution)/shard_map/while/body/eval_jaxpr/ppermute | solution.py:23
  76.2 11.7 %collective-permute-start.2 = (f32[256,512]{0,1:T(8,128)S(1)}, f32[256,512]{0,1:T(8,128)}, u32[]{:S(2)}, u32[]{:S(2)}) collective-permute-start(f32[256,512]{0,1:T(8,128)S(1)} %get-tuple-element.2276), channel_id=1, source_target_pairs={{0,2},{2,4},{4,6},{6,8},{8,10},{10,12},{12,14},{14,16},{16,18},{18... | collective-permute-start | bytes 1572872 | tf_op jit(solution)/shard_map/while/body/eval_jaxpr/ppermute | solution.py:23
  76.3 14.6 %collective-permute-start = (bf16[256,512]{0,1:T(8,128)(2,1)}, bf16[256,512]{0,1:T(8,128)(2,1)S(1)}, u32[]{:S(2)}, u32[]{:S(2)}) collective-permute-start(bf16[256,512]{0,1:T(8,128)(2,1)} %copy.127), channel_id=1, source_target_pairs={{0,2},{2,4},{4,6},{6,8},{8,10},{10,12},{12,14},{14,16},{16,18},{18... | collective-permute-start | bytes 786440 | tf_op jit(solution)/shard_map/while/body/eval_jaxpr/ppermute | solution.py:17
  78.2 15.5 %collective-permute-start.1 = (bf16[256,512]{0,1:T(8,128)(2,1)}, bf16[256,512]{0,1:T(8,128)(2,1)}, u32[]{:S(2)}, u32[]{:S(2)}) collective-permute-start(bf16[256,512]{0,1:T(8,128)(2,1)} %copy.128), channel_id=1, source_target_pairs={{0,2},{2,4},{4,6},{6,8},{8,10},{10,12},{12,14},{14,16},{16,18},{18... | collective-permute-start | bytes 786440 | tf_op jit(solution)/shard_map/while/body/eval_jaxpr/ppermute | solution.py:17
  124.0 8.6 %collective-permute-start.3 = (f32[256,512]{0,1:T(8,128)S(1)}, f32[256,512]{0,1:T(8,128)}, u32[]{:S(2)}, u32[]{:S(2)}) collective-permute-start(f32[256,512]{0,1:T(8,128)S(1)} %get-tuple-element.2277), channel_id=1, source_target_pairs={{0,2},{2,4},{4,6},{6,8},{8,10},{10,12},{12,14},{14,16},{16,18},{18... | collective-permute-start | bytes 1572872 | tf_op jit(solution)/shard_map/while/body/eval_jaxpr/ppermute | solution.py:23
  126.4 11.7 %collective-permute-start.2 = (f32[256,512]{0,1:T(8,128)S(1)}, f32[256,512]{0,1:T(8,128)}, u32[]{:S(2)}, u32[]{:S(2)}) collective-permute-start(f32[256,512]{0,1:T(8,128)S(1)} %get-tuple-element.2276), channel_id=1, source_target_pairs={{0,2},{2,4},{4,6},{6,8},{8,10},{10,12},{12,14},{14,16},{16,18},{18... | collective-permute-start | bytes 1572872 | tf_op jit(solution)/shard_map/while/body/eval_jaxpr/ppermute | solution.py:23
  126.5 14.6 %collective-permute-start = (bf16[256,512]{0,1:T(8,128)(2,1)}, bf16[256,512]{0,1:T(8,128)(2,1)S(1)}, u32[]{:S(2)}, u32[]{:S(2)}) collective-permute-start(bf16[256,512]{0,1:T(8,128)(2,1)} %copy.127), channel_id=1, source_target_pairs={{0,2},{2,4},{4,6},{6,8},{8,10},{10,12},{12,14},{14,16},{16,18},{18... | collective-permute-start | bytes 786440 | tf_op jit(solution)/shard_map/while/body/eval_jaxpr/ppermute | solution.py:17
  128.4 15.5 %collective-permute-start.1 = (bf16[256,512]{0,1:T(8,128)(2,1)}, bf16[256,512]{0,1:T(8,128)(2,1)}, u32[]{:S(2)}, u32[]{:S(2)}) collective-permute-start(bf16[256,512]{0,1:T(8,128)(2,1)} %copy.128), channel_id=1, source_target_pairs={{0,2},{2,4},{4,6},{6,8},{8,10},{10,12},{12,14},{14,16},{16,18},{18... | collective-permute-start | bytes 786440 | tf_op jit(solution)/shard_map/while/body/eval_jaxpr/ppermute | solution.py:17
  154.8 28.0 %collective-permute-start.3 = (f32[256,512]{0,1:T(8,128)S(1)}, f32[256,512]{0,1:T(8,128)}, u32[]{:S(2)}, u32[]{:S(2)}) collective-permute-start(f32[256,512]{0,1:T(8,128)S(1)} %get-tuple-element.2277), channel_id=1, source_target_pairs={{0,2},{2,4},{4,6},{6,8},{8,10},{10,12},{12,14},{14,16},{16,18},{18... | collective-permute-start | bytes 1572872 | tf_op jit(solution)/shard_map/while/body/eval_jaxpr/ppermute | solution.py:23
  176.7 11.7 %collective-permute-start.2 = (f32[256,512]{0,1:T(8,128)S(1)}, f32[256,512]{0,1:T(8,128)}, u32[]{:S(2)}, u32[]{:S(2)}) collective-permute-start(f32[256,512]{0,1:T(8,128)S(1)} %get-tuple-element.2276), channel_id=1, source_target_pairs={{0,2},{2,4},{4,6},{6,8},{8,10},{10,12},{12,14},{14,16},{16,18},{18... | collective-permute-start | bytes 1572872 | tf_op jit(solution)/shard_map/while/body/eval_jaxpr/ppermute | solution.py:23
  176.8 14.6 %collective-permute-start = (bf16[256,512]{0,1:T(8,128)(2,1)}, bf16[256,512]{0,1:T(8,128)(2,1)S(1)}, u32[]{:S(2)}, u32[]{:S(2)}) collective-permute-start(bf16[256,512]{0,1:T(8,128)(2,1)} %copy.127), channel_id=1, source_target_pairs={{0,2},{2,4},{4,6},{6,8},{8,10},{10,12},{12,14},{14,16},{16,18},{18... | collective-permute-start | bytes 786440 | tf_op jit(solution)/shard_map/while/body/eval_jaxpr/ppermute | solution.py:17
  178.7 15.5 %collective-permute-start.1 = (bf16[256,512]{0,1:T(8,128)(2,1)}, bf16[256,512]{0,1:T(8,128)(2,1)}, u32[]{:S(2)}, u32[]{:S(2)}) collective-permute-start(bf16[256,512]{0,1:T(8,128)(2,1)} %copy.128), channel_id=1, source_target_pairs={{0,2},{2,4},{4,6},{6,8},{8,10},{10,12},{12,14},{14,16},{16,18},{18... | collective-permute-start | bytes 786440 | tf_op jit(solution)/shard_map/while/body/eval_jaxpr/ppermute | solution.py:17
  205.0 22.2 %collective-permute-start.3 = (f32[256,512]{0,1:T(8,128)S(1)}, f32[256,512]{0,1:T(8,128)}, u32[]{:S(2)}, u32[]{:S(2)}) collective-permute-start(f32[256,512]{0,1:T(8,128)S(1)} %get-tuple-element.2277), channel_id=1, source_target_pairs={{0,2},{2,4},{4,6},{6,8},{8,10},{10,12},{12,14},{14,16},{16,18},{18... | collective-permute-start | bytes 1572872 | tf_op jit(solution)/shard_map/while/body/eval_jaxpr/ppermute | solution.py:23
  207.6 20.7 %collective-permute-start.2 = (f32[256,512]{0,1:T(8,128)S(1)}, f32[256,512]{0,1:T(8,128)}, u32[]{:S(2)}, u32[]{:S(2)}) collective-permute-start(f32[256,512]{0,1:T(8,128)S(1)} %get-tuple-element.2276), channel_id=1, source_target_pairs={{0,2},{2,4},{4,6},{6,8},{8,10},{10,12},{12,14},{14,16},{16,18},{18... | collective-permute-start | bytes 1572872 | tf_op jit(solution)/shard_map/while/body/eval_jaxpr/ppermute | solution.py:23
  221.0 9.0 %collective-permute-start = (bf16[256,512]{0,1:T(8,128)(2,1)}, bf16[256,512]{0,1:T(8,128)(2,1)S(1)}, u32[]{:S(2)}, u32[]{:S(2)}) collective-permute-start(bf16[256,512]{0,1:T(8,128)(2,1)} %copy.127), channel_id=1, source_target_pairs={{0,2},{2,4},{4,6},{6,8},{8,10},{10,12},{12,14},{14,16},{16,18},{18... | collective-permute-start | bytes 786440 | tf_op jit(solution)/shard_map/while/body/eval_jaxpr/ppermute | solution.py:17
  223.0 9.9 %collective-permute-start.1 = (bf16[256,512]{0,1:T(8,128)(2,1)}, bf16[256,512]{0,1:T(8,128)(2,1)}, u32[]{:S(2)}, u32[]{:S(2)}) collective-permute-start(bf16[256,512]{0,1:T(8,128)(2,1)} %copy.128), channel_id=1, source_target_pairs={{0,2},{2,4},{4,6},{6,8},{8,10},{10,12},{12,14},{14,16},{16,18},{18... | collective-permute-start | bytes 786440 | tf_op jit(solution)/shard_map/while/body/eval_jaxpr/ppermute | solution.py:17
  243.7 54.1 %collective-permute-start.3 = (f32[256,512]{0,1:T(8,128)S(1)}, f32[256,512]{0,1:T(8,128)}, u32[]{:S(2)}, u32[]{:S(2)}) collective-permute-start(f32[256,512]{0,1:T(8,128)S(1)} %get-tuple-element.2277), channel_id=1, source_target_pairs={{0,2},{2,4},{4,6},{6,8},{8,10},{10,12},{12,14},{14,16},{16,18},{18... | collective-permute-start | bytes 1572872 | tf_op jit(solution)/shard_map/while/body/eval_jaxpr/ppermute | solution.py:23
  251.8 47.0 %collective-permute-start.2 = (f32[256,512]{0,1:T(8,128)S(1)}, f32[256,512]{0,1:T(8,128)}, u32[]{:S(2)}, u32[]{:S(2)}) collective-permute-start(f32[256,512]{0,1:T(8,128)S(1)} %get-tuple-element.2276), channel_id=1, source_target_pairs={{0,2},{2,4},{4,6},{6,8},{8,10},{10,12},{12,14},{14,16},{16,18},{18... | collective-permute-start | bytes 1572872 | tf_op jit(solution)/shard_map/while/body/eval_jaxpr/ppermute | solution.py:23
  265.4 34.5 %collective-permute-start = (bf16[256,512]{0,1:T(8,128)(2,1)}, bf16[256,512]{0,1:T(8,128)(2,1)S(1)}, u32[]{:S(2)}, u32[]{:S(2)}) collective-permute-start(bf16[256,512]{0,1:T(8,128)(2,1)} %copy.127), channel_id=1, source_target_pairs={{0,2},{2,4},{4,6},{6,8},{8,10},{10,12},{12,14},{14,16},{16,18},{18... | collective-permute-start | bytes 786440 | tf_op jit(solution)/shard_map/while/body/eval_jaxpr/ppermute | solution.py:17
  291.2 10.1 %collective-permute-start.1 = (bf16[256,512]{0,1:T(8,128)(2,1)}, bf16[256,512]{0,1:T(8,128)(2,1)}, u32[]{:S(2)}, u32[]{:S(2)}) collective-permute-start(bf16[256,512]{0,1:T(8,128)(2,1)} %copy.128), channel_id=1, source_target_pairs={{0,2},{2,4},{4,6},{6,8},{8,10},{10,12},{12,14},{14,16},{16,18},{18... | collective-permute-start | bytes 786440 | tf_op jit(solution)/shard_map/while/body/eval_jaxpr/ppermute | solution.py:17
  312.2 43.2 %collective-permute-start.3 = (f32[256,512]{0,1:T(8,128)S(1)}, f32[256,512]{0,1:T(8,128)}, u32[]{:S(2)}, u32[]{:S(2)}) collective-permute-start(f32[256,512]{0,1:T(8,128)S(1)} %get-tuple-element.2277), channel_id=1, source_target_pairs={{0,2},{2,4},{4,6},{6,8},{8,10},{10,12},{12,14},{14,16},{16,18},{18... | collective-permute-start | bytes 1572872 | tf_op jit(solution)/shard_map/while/body/eval_jaxpr/ppermute | solution.py:23
  321.4 35.1 %collective-permute-start.2 = (f32[256,512]{0,1:T(8,128)S(1)}, f32[256,512]{0,1:T(8,128)}, u32[]{:S(2)}, u32[]{:S(2)}) collective-permute-start(f32[256,512]{0,1:T(8,128)S(1)} %get-tuple-element.2276), channel_id=1, source_target_pairs={{0,2},{2,4},{4,6},{6,8},{8,10},{10,12},{12,14},{14,16},{16,18},{18... | collective-permute-start | bytes 1572872 | tf_op jit(solution)/shard_map/while/body/eval_jaxpr/ppermute | solution.py:23
  335.0 22.6 %collective-permute-start = (bf16[256,512]{0,1:T(8,128)(2,1)}, bf16[256,512]{0,1:T(8,128)(2,1)S(1)}, u32[]{:S(2)}, u32[]{:S(2)}) collective-permute-start(bf16[256,512]{0,1:T(8,128)(2,1)} %copy.127), channel_id=1, source_target_pairs={{0,2},{2,4},{4,6},{6,8},{8,10},{10,12},{12,14},{14,16},{16,18},{18... | collective-permute-start | bytes 786440 | tf_op jit(solution)/shard_map/while/body/eval_jaxpr/ppermute | solution.py:17
  341.5 17.6 %collective-permute-start.1 = (bf16[256,512]{0,1:T(8,128)(2,1)}, bf16[256,512]{0,1:T(8,128)(2,1)}, u32[]{:S(2)}, u32[]{:S(2)}) collective-permute-start(bf16[256,512]{0,1:T(8,128)(2,1)} %copy.128), channel_id=1, source_target_pairs={{0,2},{2,4},{4,6},{6,8},{8,10},{10,12},{12,14},{14,16},{16,18},{18... | collective-permute-start | bytes 786440 | tf_op jit(solution)/shard_map/while/body/eval_jaxpr/ppermute | solution.py:17
  369.9 29.6 %collective-permute-start.3 = (f32[256,512]{0,1:T(8,128)S(1)}, f32[256,512]{0,1:T(8,128)}, u32[]{:S(2)}, u32[]{:S(2)}) collective-permute-start(f32[256,512]{0,1:T(8,128)S(1)} %get-tuple-element.2277), channel_id=1, source_target_pairs={{0,2},{2,4},{4,6},{6,8},{8,10},{10,12},{12,14},{14,16},{16,18},{18... | collective-permute-start | bytes 1572872 | tf_op jit(solution)/shard_map/while/body/eval_jaxpr/ppermute | solution.py:23
  372.5 28.1 %collective-permute-start.2 = (f32[256,512]{0,1:T(8,128)S(1)}, f32[256,512]{0,1:T(8,128)}, u32[]{:S(2)}, u32[]{:S(2)}) collective-permute-start(f32[256,512]{0,1:T(8,128)S(1)} %get-tuple-element.2276), channel_id=1, source_target_pairs={{0,2},{2,4},{4,6},{6,8},{8,10},{10,12},{12,14},{14,16},{16,18},{18... | collective-permute-start | bytes 1572872 | tf_op jit(solution)/shard_map/while/body/eval_jaxpr/ppermute | solution.py:23
  388.9 12.8 %collective-permute-start = (bf16[256,512]{0,1:T(8,128)(2,1)}, bf16[256,512]{0,1:T(8,128)(2,1)S(1)}, u32[]{:S(2)}, u32[]{:S(2)}) collective-permute-start(bf16[256,512]{0,1:T(8,128)(2,1)} %copy.127), channel_id=1, source_target_pairs={{0,2},{2,4},{4,6},{6,8},{8,10},{10,12},{12,14},{14,16},{16,18},{18... | collective-permute-start | bytes 786440 | tf_op jit(solution)/shard_map/while/body/eval_jaxpr/ppermute | solution.py:17
  414.0 29.7 %collective-permute-start.3 = (f32[256,512]{0,1:T(8,128)S(1)}, f32[256,512]{0,1:T(8,128)}, u32[]{:S(2)}, u32[]{:S(2)}) collective-permute-start(f32[256,512]{0,1:T(8,128)S(1)} %get-tuple-element.2277), channel_id=1, source_target_pairs={{0,2},{2,4},{4,6},{6,8},{8,10},{10,12},{12,14},{14,16},{16,18},{18... | collective-permute-start | bytes 1572872 | tf_op jit(solution)/shard_map/while/body/eval_jaxpr/ppermute | solution.py:23
  416.6 28.2 %collective-permute-start.2 = (f32[256,512]{0,1:T(8,128)S(1)}, f32[256,512]{0,1:T(8,128)}, u32[]{:S(2)}, u32[]{:S(2)}) collective-permute-start(f32[256,512]{0,1:T(8,128)S(1)} %get-tuple-element.2276), channel_id=1, source_target_pairs={{0,2},{2,4},{4,6},{6,8},{8,10},{10,12},{12,14},{14,16},{16,18},{18... | collective-permute-start | bytes 1572872 | tf_op jit(solution)/shard_map/while/body/eval_jaxpr/ppermute | solution.py:23
  423.2 22.5 %collective-permute-start = (bf16[256,512]{0,1:T(8,128)(2,1)}, bf16[256,512]{0,1:T(8,128)(2,1)S(1)}, u32[]{:S(2)}, u32[]{:S(2)}) collective-permute-start(bf16[256,512]{0,1:T(8,128)(2,1)} %copy.127), channel_id=1, source_target_pairs={{0,2},{2,4},{4,6},{6,8},{8,10},{10,12},{12,14},{14,16},{16,18},{18... | collective-permute-start | bytes 786440 | tf_op jit(solution)/shard_map/while/body/eval_jaxpr/ppermute | solution.py:17
  455.8 91.4 %collective-permute-start.4 = (bf16[256,512]{1,0:T(8,128)(2,1)S(1)}, bf16[256,512]{1,0:T(8,128)(2,1)S(1)}, u32[]{:S(2)}, u32[]{:S(2)}) collective-permute-start(bf16[256,512]{1,0:T(8,128)(2,1)S(1)} %copy.51), channel_id=1, source_target_pairs={{0,112},{2,114},{4,116},{6,118},{8,120},{10,122},{12,124},{14,126}... | collective-permute-start | bytes 786440 | tf_op jit(solution)/shard_map/ppermute | solution.py:23
  492.7 57.4 %collective-permute-start.5 = (bf16[256,512]{1,0:T(8,128)(2,1)S(1)}, bf16[256,512]{1,0:T(8,128)(2,1)S(1)}, u32[]{:S(2)}, u32[]{:S(2)}) collective-permute-start(bf16[256,512]{1,0:T(8,128)(2,1)S(1)} %copy.52), channel_id=1, source_target_pairs={{0,112},{2,114},{4,116},{6,118},{8,120},{10,122},{12,124},{14,126}... | collective-permute-start | bytes 786440 | tf_op jit(solution)/shard_map/ppermute | solution.py:23
  (14 other events, 33.0 us)
where the time goes:
time: 556 us; the launch traced here: 552 us
  starting transfers between devices  261 us (47%)
  local copies, waits for them, and re-layouts  132 us (24%)
  waiting for transfers between devices  89.7 us (16%)
  loops' own time  27.6 us (5%)
  other arithmetic  21.2 us (4%)
  matrix products  19 us (3%)
    ppermute x18, starting transfers between devices, passed_along(): return lax.ppermute(value, axis, pairs)  159 us
    ppermute x16, starting transfers between devices, shifted(): lax.ppermute(value, axis, [(source, source + steps) for source in range(f...  102 us
    ppermute x18, waiting for transfers between devices, passed_along(): return lax.ppermute(value, axis, pairs)  66.2 us
    while x48, local copies, waits for them, and re-layouts  58.9 us
    unnamed x16, local copies, waits for them, and re-layouts  30.4 us
    another operation x9, loops' own time, grad_update(): return lax.fori_loop(0, blocks * blocks, one_pair, grad_sums)  26.2 us
    ppermute x16, waiting for transfers between devices, shifted(): lax.ppermute(value, axis, [(source, source + steps) for source in range(f...  23.6 us
    dynamic_slice x36, local copies, waits for them, and re-layouts, pair_setup(): flag_value = active[query_part, jnp.clip(distance, 0, WINBLK - 1)]  23.4 us
  transfers between devices with their start and end apart: 34, of which 20 were waited for; matrix products, arithmetic and copies ran while one was open for 4% of the time, Pallas kernels for 0%

commit v1 on v0

v1 whole, which is shorter than its diff:
```python
import functools

import jax
import jax.numpy as jnp
from jax import lax
from jax.experimental import pallas as pl
from jax.experimental.pallas import tpu as pltpu
from jax.sharding import PartitionSpec as P

D = 128
BLK = 128
WIN = 16
CTX = 64
TOK = 256
CHIP = 512
HALF = 2048
NSEG = 16
FACTOR = D ** -0.5
LOG2E = 1.4426950408889634
LOWEST = -1.0e30
F32, BF16, I32 = jnp.float32, jnp.bfloat16, jnp.int32
MESH = pl.DeviceIdType.MESH
NT = (((1,), (1,)), ((), ()))
NN = (((1,), (0,)), ((), ()))
TN = (((0,), (0,)), ((), ()))


def dot(left, right, dims):
    return lax.dot_general(left, right, dims, preferred_element_type=F32)


class Place:
    def __init__(self):
        self.ctx = lax.axis_index("ctx")
        self.kvh = lax.axis_index("kvh")
        self.core = lax.rem(self.ctx, 2)
        self.chip = lax.div(self.ctx, 2)
        self.x = lax.rem(self.chip, 4)

    def sibling(self):
        return (self.ctx + 1 - 2 * self.core, self.kvh)

    def later(self, k):
        x = lax.rem(self.x + k, 4)
        return (self.ctx + 2 * (x - self.x), self.kvh)

    def line(self, step):
        return (lax.rem(self.ctx + CTX + 8 * step, CTX), self.kvh)


def enter(place):
    barrier = pltpu.get_barrier_semaphore()
    peers = [place.sibling(), place.later(1), place.later(2), place.later(3), place.line(1), place.line(-1)]
    for peer in peers:
        pl.semaphore_signal(barrier, inc=1, device_id=peer, device_id_type=MESH)
    pl.semaphore_wait(barrier, len(peers))


def remote(src, dst, send, recv, peer):
    return pltpu.make_async_remote_copy(
        src_ref=src, dst_ref=dst, send_sem=send, recv_sem=recv, device_id=peer, device_id_type=MESH
    )


def gather_kernel(q, k, v, o, lse, do, seg, act,
                  kv, qsib, dosib, rows, starts, act0, act1,
                  mine, theirs, actin, actbuf,
                  own_l, pair_s, pair_r, up_s, up_r, line_s, line_r, big_s, big_r, small_s, small_r):
    place = Place()
    core, x = place.core, place.x
    other = 1 - core
    enter(place)
    sib = place.sibling()

    def part(piece, half):
        source = (k, v)[piece % 2]
        return source.at[:, pl.ds(pl.multiple_of((half * 2 + piece // 2) * D, D), D)]

    def shelf(slot, piece):
        return kv.at[slot, piece]

    local, pair = [], []
    for p in range(4):
        dst = kv.at[4, p, pl.ds(pl.multiple_of(core * TOK, TOK), TOK), :]
        pair.append(remote(part(p, other), dst, pair_s.at[p], pair_r.at[p], sib))
        local.append(pltpu.make_async_copy(part(p, core), dst, own_l.at[p]))
        pair[p].start()
        local[p].start()
    away = pl.ds(pl.multiple_of(other * HALF, HALF), HALF)
    big = [remote(do.at[:, away], dosib, big_s.at[0], big_r.at[0], sib),
           remote(q.at[:, away], qsib, big_s.at[1], big_r.at[1], sib)]
    for copy in big:
        copy.start()
    actin[...] = jnp.zeros_like(actin)
    actin[0:2, 0:WIN] = act[...]
    small = [remote(actin, actbuf, small_s.at[0], small_r.at[0], sib)]
    small[0].start()

    up = [remote(shelf(4, p), shelf(0, p), up_s.at[p], up_r.at[p], place.line(1)) for p in range(4)]
    own_line = [[remote(shelf(4, p), shelf(4 - s, p), line_s.at[s - 1, p], line_r.at[s - 1, p], place.later(s))
                 for p in range(4)] for s in (1, 2, 3)]
    prev_line = [[remote(shelf(0, p), shelf(4 - s, p), line_s.at[s - 1, p], line_r.at[s - 1, p], place.later(s))
                  for p in range(4)] for s in (1, 2, 3)]
    for p in range(4):
        local[p].wait()
        pair[p].wait()
        up[p].start()
        for s in (1, 2, 3):
            @pl.when(x + s < 4)
            def _(s=s, p=p):
                own_line[s - 1][p].start()

    spread = jnp.where(lax.broadcasted_iota(I32, (8, 8 * D), 1) // D == lax.broadcasted_iota(I32, (8, 8 * D), 0),
                       1.0, 0.0).astype(BF16)
    for g in range(4):
        cols = slice(g * 8 * D, (g + 1) * 8 * D)
        product = do[:, cols].astype(F32) * o[:, cols].astype(F32)
        high = product.astype(BF16)
        low = (product - high.astype(F32)).astype(BF16)
        delta = dot(spread, high, NT) + dot(spread, low, NT)
        logs = lse[g * 8:(g + 1) * 8, :] * LOG2E

        @pl.when(core == g // 2)
        def _(delta=delta, logs=logs, g=g):
            mine[0, g % 2] = logs
            mine[1, g % 2] = delta

        @pl.when(core != g // 2)
        def _(delta=delta, logs=logs, g=g):
            theirs[0, g % 2] = logs
            theirs[1, g % 2] = delta

    small.append(remote(theirs, rows.at[core], small_s.at[1], small_r.at[1], sib))
    small[1].start()
    place_rows = pltpu.make_async_copy(mine, rows.at[core], own_l.at[4])

    seg_all = seg[...]
    seg_here = seg[pl.ds(place.chip * 4, 4), :]
    first = jnp.zeros((4, BLK), I32)
    for s in range(1, NSEG):
        first = jnp.where(seg_here == s, jnp.sum((seg_all < s).astype(I32)), first)
    starts[...] = jnp.zeros_like(starts)
    starts[0:4, :] = first

    for p in range(4):
        up[p].wait_recv()
        for s in (1, 2, 3):
            @pl.when(x + s >= 4)
            def _(s=s, p=p):
                prev_line[s - 1][p].start()
    for p in range(4):
        up[p].wait_send()
        for s in (1, 2, 3):
            own_line[s - 1][p].wait()
    for copy in big + small:
        copy.wait()
    place_rows.start()
    place_rows.wait()

    @pl.when(core == 0)
    def _():
        act0[...] = actin[...]
        act1[...] = actbuf[...]

    @pl.when(core == 1)
    def _():
        act0[...] = actbuf[...]
        act1[...] = actin[...]


def gather(q, k, v, o, lse, do, seg, act):
    anywhere = pl.BlockSpec(memory_space=pl.ANY)
    vmem = pl.BlockSpec(memory_space=pltpu.VMEM)
    dma = pltpu.SemaphoreType.DMA
    return pl.pallas_call(
        gather_kernel,
        out_shape=[
            jax.ShapeDtypeStruct((5, 4, CHIP, D), BF16),
            jax.ShapeDtypeStruct((TOK, HALF), BF16),
            jax.ShapeDtypeStruct((TOK, HALF), BF16),
            jax.ShapeDtypeStruct((2, 2, 2, 8, TOK), F32),
            jax.ShapeDtypeStruct((8, BLK), I32),
            jax.ShapeDtypeStruct((8, BLK), I32),
            jax.ShapeDtypeStruct((8, BLK), I32),
        ],
        in_specs=[anywhere, anywhere, anywhere, vmem, vmem, vmem, vmem, vmem],
        out_specs=[anywhere, anywhere, anywhere, anywhere, vmem, vmem, vmem],
        scratch_shapes=[
            pltpu.VMEM((2, 2, 8, TOK), F32),
            pltpu.VMEM((2, 2, 8, TOK), F32),
            pltpu.VMEM((8, BLK), I32),
            pltpu.VMEM((8, BLK), I32),
            dma((5,)), dma((4,)), dma((4,)), dma((4,)), dma((4,)), dma((3, 4)), dma((3, 4)),
            dma((2,)), dma((2,)), dma((2,)), dma((2,)),
        ],
        compiler_params=pltpu.CompilerParams(
            collective_id=0, has_side_effects=True, vmem_limit_bytes=63 * 2 ** 20),
        name="gather",
    )(q, k, v, o, lse, do, seg, act)


def compute_kernel(starts_s, act0, act1, starts_v, rows, kv, q, do, qsib, dosib,
                   parts, own, dq,
                   qv, dov, dq_sum, kv_sum, list_q, list_k, sems):
    core = lax.rem(lax.axis_index("ctx"), 2)
    chip = lax.div(lax.axis_index("ctx"), 2)
    here = pl.ds(pl.multiple_of(core * HALF, HALF), HALF)
    mine = pl.ds(pl.multiple_of(core * TOK, TOK), TOK)
    theirs = pl.ds(pl.multiple_of((1 - core) * TOK, TOK), TOK)
    loads = [
        pltpu.make_async_copy(q.at[:, here], qv.at[mine, :], sems.at[0]),
        pltpu.make_async_copy(qsib, qv.at[theirs, :], sems.at[1]),
        pltpu.make_async_copy(do.at[:, here], dov.at[mine, :], sems.at[2]),
        pltpu.make_async_copy(dosib, dov.at[theirs, :], sems.at[3]),
    ]
    for copy in loads:
        copy.start()

    count = jnp.int32(0)
    for a in range(4):
        first = starts_s[a, 0]
        flags = (act0, act1)[a // 2]

        def consider(d, count, a=a, first=first, flags=flags):
            reach = ((chip * 4 + a - d) * BLK + (BLK - 1) >= first) & (flags[a % 2, d] > 0)
            list_q[count] = a
            list_k[count] = 16 + a - d
            return count + reach.astype(I32)

        count = lax.fori_loop(0, WIN, consider, count)
    list_q[count] = 0
    list_k[count] = 16

    dq_sum[...] = jnp.zeros_like(dq_sum)
    kv_sum[...] = jnp.zeros_like(kv_sum)
    for copy in loads:
        copy.wait()

    key_at = lax.broadcasted_iota(I32, (BLK, BLK), 0)
    query_at = lax.broadcasted_iota(I32, (1, BLK), 1)

    def chain(entry):
        a, rel = list_q[entry], list_k[entry]
        slot, block = lax.div(rel, 4), lax.rem(rel, 4)
        offset = pl.multiple_of(block * BLK, BLK)
        keys = pl.ds(offset, BLK)
        tokens = pl.ds(pl.multiple_of(a * BLK, BLK), BLK)
        base = (chip * 4 - 16 + rel) * BLK
        first = jnp.where(entry < count, starts_v[pl.ds(a, 1), :], 2 ** 30) - base
        last = (chip * 4 + a) * BLK + query_at - base
        bias = jnp.where((key_at >= first) & (key_at <= last), 0.0, LOWEST)
        for g in range(2):
            key, value = kv[slot, 2 * g, keys, :], kv[slot, 2 * g + 1, keys, :]
            columns = [slice((g * 8 + j) * D, (g * 8 + j + 1) * D) for j in range(8)]
            query = jnp.concatenate([qv[tokens, c] for c in columns], 0)
            cotangent = jnp.concatenate([dov[tokens, c] for c in columns], 0)
            scores = dot(key, query, NT)
            grad_weights = dot(value, cotangent, NT)
            half = lax.div(a, 2)
            lanes = pl.ds(pl.multiple_of(lax.rem(a, 2) * BLK, BLK), BLK)
            weights, grad_scores = [], []
            for j in range(8):
                lane = slice(j * BLK, (j + 1) * BLK)
                log_row = rows[half, 0, g, j:j + 1, lanes]
                delta_row = rows[half, 1, g, j:j + 1, lanes]
                weight = jnp.exp2(scores[:, lane] * (FACTOR * LOG2E) - log_row + bias)
                weights.append(weight.astype(BF16))
                grad_scores.append((weight * (grad_weights[:, lane] - delta_row)).astype(BF16))
            weights = jnp.concatenate(weights, 1)
            grad_scores = jnp.concatenate(grad_scores, 1)
            kv_sum[slot, 2 * g, keys, :] += dot(grad_scores, query, NN)
            kv_sum[slot, 2 * g + 1, keys, :] += dot(weights, cotangent, NN)
            dq_sum[a, g] += dot(key, grad_scores, TN)

    def step(i, carry):
        chain(2 * i)
        chain(2 * i + 1)
        return carry

    lax.fori_loop(0, lax.div(count + 1, 2), step, 0)

    for p in range(4):
        scale = FACTOR if p % 2 == 0 else 1.0
        for s in range(4):
            parts[s, p] = (kv_sum[s, p] * scale).astype(BF16)
        own[p] = kv_sum[4, p] * scale

    def turn(i, carry):
        a, g = lax.div(i, 2), lax.rem(i, 2)
        tokens = pl.ds(pl.multiple_of(a * BLK, BLK), BLK)
        for j in range(8):
            block = dq_sum[a, g, :, j * BLK:(j + 1) * BLK].T * FACTOR
            dq[tokens, pl.ds(pl.multiple_of((g * 8 + j) * D, D), D)] = block.astype(BF16)
        return carry

    lax.fori_loop(0, 8, turn, 0)


def compute(starts, act0, act1, rows, kv, q, do, qsib, dosib):
    anywhere = pl.BlockSpec(memory_space=pl.ANY)
    vmem = pl.BlockSpec(memory_space=pltpu.VMEM)
    smem = pl.BlockSpec(memory_space=pltpu.SMEM)
    return pl.pallas_call(
        compute_kernel,
        out_shape=[
            jax.ShapeDtypeStruct((4, 4, CHIP, D), BF16),
            jax.ShapeDtypeStruct((4, CHIP, D), F32),
            jax.ShapeDtypeStruct((CHIP, HALF), BF16),
        ],
        in_specs=[smem, smem, smem, vmem, vmem, vmem, anywhere, anywhere, anywhere, anywhere],
        out_specs=[vmem, vmem, vmem],
        scratch_shapes=[
            pltpu.VMEM((CHIP, HALF), BF16),
            pltpu.VMEM((CHIP, HALF), BF16),
            pltpu.VMEM((4, 2, D, 8 * BLK), F32),
            pltpu.VMEM((5, 4, CHIP, D), F32),
            pltpu.SMEM((72,), I32),
            pltpu.SMEM((72,), I32),
            pltpu.SemaphoreType.DMA((4,)),
        ],
        compiler_params=pltpu.CompilerParams(vmem_limit_bytes=63 * 2 ** 20),
        name="compute",
    )(starts, act0, act1, starts, rows, kv, q, do, qsib, dosib)


def return_kernel(parts, own, dq,
                  gq, gk, gv,
                  far, got, relay, total, final,
                  load_s, line_s, line_r, up_s, up_r, out_s, fin_s, fin_r, q_s, q_r):
    place = Place()
    core, x = place.core, place.x
    other = 1 - core
    here = pl.ds(pl.multiple_of(core * HALF, HALF), HALF)
    mine = pl.ds(pl.multiple_of(core * TOK, TOK), TOK)
    theirs = pl.ds(pl.multiple_of(other * TOK, TOK), TOK)
    loads = [pltpu.make_async_copy(parts.at[0], far, load_s.at[0]),
             pltpu.make_async_copy(own, total, load_s.at[1])]
    for copy in loads:
        copy.start()
    enter(place)
    sib = place.sibling()
    line = [[remote(parts.at[4 - s, p], got.at[s - 1, p], line_s.at[s - 1, p], line_r.at[s - 1, p], place.later(4 - s))
             for p in range(4)] for s in (1, 2, 3)]
    for p in range(4):
        for s in (1, 2, 3):
            @pl.when(x - s < 0)
            def _(s=s, p=p):
                line[s - 1][p].start()
    for p in range(4):
        for s in (1, 2, 3):
            @pl.when(x - s >= 0)
            def _(s=s, p=p):
                line[s - 1][p].start()
    send_q = remote(dq.at[theirs, :], gq.at[:, here], q_s.at[0], q_r.at[0], sib)
    send_q.start()
    keep_q = pltpu.make_async_copy(dq.at[mine, :], gq.at[:, here], load_s.at[2])
    keep_q.start()
    for copy in loads:
        copy.wait()

    up = [remote(relay.at[p], got.at[3, p], up_s.at[p], up_r.at[p], place.line(-1)) for p in range(4)]
    for p in range(4):
        summed = far[p].astype(F32)
        final[...] = summed
        for s in (3, 2, 1):
            @pl.when(x + s >= 4)
            def _(s=s, p=p):
                line[s - 1][p].wait_recv()
                final[...] += got[s - 1, p].astype(F32)
        relay[p] = final[...].astype(BF16)
        up[p].start()
    finish = []
    for p in range(4):
        for s in (1, 2, 3):
            @pl.when(x + s < 4)
            def _(s=s, p=p):
                line[s - 1][p].wait_recv()
                total[p] += got[s - 1, p].astype(F32)
    for p in range(4):
        up[p].wait_recv()
        far[p] = (total[p] + got[3, p].astype(F32)).astype(BF16)
        columns = pl.ds(pl.multiple_of((core * 2 + p // 2) * D, D), D)
        target = (gk, gv)[p % 2].at[:, columns]
        finish.append(remote(far.at[p, theirs, :], target, fin_s.at[p], fin_r.at[p], sib))
        finish[p].start()
        keep = pltpu.make_async_copy(far.at[p, mine, :], target, out_s.at[p])
        keep.start()
    for p in range(4):
        pltpu.make_async_copy(
            far.at[p, mine, :],
            (gk, gv)[p % 2].at[:, pl.ds(pl.multiple_of((core * 2 + p // 2) * D, D), D)], out_s.at[p]).wait()
        finish[p].wait()
        up[p].wait_send()
        for s in (1, 2, 3):
            line[s - 1][p].wait_send()
    send_q.wait()
    keep_q.wait()


def give_back(parts, own, dq):
    anywhere = pl.BlockSpec(memory_space=pl.ANY)
    dma = pltpu.SemaphoreType.DMA
    return pl.pallas_call(
        return_kernel,
        out_shape=[
            jax.ShapeDtypeStruct((TOK, 2 * HALF), BF16),
            jax.ShapeDtypeStruct((TOK, 4 * D), BF16),
            jax.ShapeDtypeStruct((TOK, 4 * D), BF16),
        ],
        in_specs=[anywhere] * 3,
        out_specs=[anywhere] * 3,
        scratch_shapes=[
            pltpu.VMEM((4, CHIP, D), BF16),
            pltpu.VMEM((4, 4, CHIP, D), BF16),
            pltpu.VMEM((4, CHIP, D), BF16),
            pltpu.VMEM((4, CHIP, D), F32),
            pltpu.VMEM((CHIP, D), F32),
            dma((3,)), dma((3, 4)), dma((3, 4)), dma((4,)), dma((4,)), dma((4,)), dma((4,)), dma((4,)),
            dma((1,)), dma((1,)),
        ],
        compiler_params=pltpu.CompilerParams(
            collective_id=1, has_side_effects=True, vmem_limit_bytes=63 * 2 ** 20),
        name="give_back",
    )(parts, own, dq)


def body(queries, keys, values, fwd_out, log_sum, out_grad, seg_ids, active):
    seg = seg_ids.reshape(TOK // 2, BLK)
    kv, qsib, dosib, rows, starts, act0, act1 = gather(
        queries, keys, values, fwd_out, log_sum, out_grad, seg, active)
    parts, own, dq = compute(starts, act0, act1, rows, kv, queries, out_grad, qsib, dosib)
    return tuple(give_back(parts, own, dq))


def solution(mesh):
    placed = (
        P("ctx", "kvh"), P("ctx", "kvh"), P("ctx", "kvh"), P("ctx", "kvh"),
        P("kvh", "ctx"), P("ctx", "kvh"), P(), P("ctx", None),
    )
    return jax.shard_map(
        body, mesh=mesh, in_specs=placed,
        out_specs=(P("ctx", "kvh"), P("ctx", "kvh"), P("ctx", "kvh")),
        check_vma=False,
    )
```

time: 556 us -> 127 us (0.23)
  the two profiles are of different devices: /device:TPU:1 before, /device:TPU:12 now
where the time goes in v1:
time: 127 us
  Pallas kernels  121 us (95%)
  local copies, waits for them, and re-layouts  4.6 us (4%)
    pallas_call x1, Pallas kernels, give_back(): pl.pallas_call(return_kernel, out_shape=[jax.ShapeDtypeStruct((TOK, 2 * H...  57.4 us
    pallas_call x1, Pallas kernels, gather(): pl.pallas_call(gather_kernel, out_shape=[jax.ShapeDtypeStruct((5, 4, CHIP...  44.3 us
    pallas_call x1, Pallas kernels, compute(): pl.pallas_call(compute_kernel, out_shape=[jax.ShapeDtypeStruct((4, 4, CHI...  19.5 us
    unnamed x7, local copies, waits for them, and re-layouts  4.6 us

profile of v1, /device:TPU:12, one launch (start us, length us, event | category | flops | bytes accessed | tf_op | source)
XLA Modules:
  0.0 126.5 jit_solution(16621188553453563765)
XLA Ops:
  0.6 44.3 %gather.1 = (bf16[5,4,512,128]{3,2,1,0:T(8,128)(2,1)}, bf16[256,2048]{1,0:T(8,128)(2,1)}, bf16[256,2048]{1,0:T(8,128)(2,1)}, f32[2,2,2,8,256]{4,3,2,1,0:T(8,128)...) custom-call(bf16[256,4096]{1,0:T(8,128)(2,1)} %q.3, bf16[256,512]{1,0:T(8,128)(2,1)} %k.1, ...), custom_call_target="tpu_custom_call" | custom-call | tf_op jit(solution)/shard_map/gather/pallas_call | solution.py:175
  45.0 19.5 %compute.1 = (bf16[4,4,512,128]{3,2,1,0:T(8,128)(2,1)}, f32[4,512,128]{2,1,0:T(8,128)}, bf16[512,2048]{1,0:T(8,128)(2,1)}) custom-call(s32[8,128]{1,0:T(8,128)} %get-tuple-element.13.starts_s.starts_v, s32[8,128]{1,0:T(8,128)} %get-tuple-element.14.act0, s32[8,128]{1,0:T(8,128)} %get-tuple-element.15.act1, s32[8,128]{1,0:T(8,128)} %get-tuple-element.13.starts_s.starts_v, ...), custom_call_target="tpu_custom_call" | custom-call | tf_op jit(solution)/shard_map/compute/pallas_call | solution.py:303
  64.5 57.4 %give_back.1 = (bf16[256,4096]{1,0:T(8,128)(2,1)}, bf16[256,512]{1,0:T(8,128)(2,1)}, bf16[256,512]{1,0:T(8,128)(2,1)}) custom-call(bf16[4,4,512,128]{3,2,1,0:T(8,128)(2,1)} %get-tuple-element.20.parts, f32[4,512,128]{2,1,0:T(8,128)} %get-tuple-element.21.own, bf16[512,2048]{1,0:T(8,128)(2,1)} %get-tuple-element.22.dq), custom_call_target="tpu_custom_call" | custom-call | tf_op jit(solution)/shard_map/give_back/pallas_call | solution.py:403
  121.9 0.0 copy-start.1
  121.9 0.0 copy-start
  121.9 3.2 %copy.14 = bf16[256,4096]{1,0:T(8,128)(2,1)} copy(bf16[256,4096]{1,0:T(8,128)(2,1)} %get-tuple-element.26) | data formatting | bytes 4194304
  125.1 0.0 copy-done.1
  125.1 0.7 copy.15
  125.8 0.0 copy-done
  125.8 0.7 copy.16
Async XLA Ops:
  121.9 3.2 %copy-start.1 = (bf16[256,512]{1,0:T(8,128)(2,1)S(1)}, bf16[256,512]{1,0:T(8,128)(2,1)}, u32[]{:S(2)}) copy-start(bf16[256,512]{1,0:T(8,128)(2,1)} %get-tuple-element.27) | copy-start | bytes 786436
  121.9 3.9 %copy-start = (bf16[256,512]{1,0:T(8,128)(2,1)S(1)}, bf16[256,512]{1,0:T(8,128)(2,1)}, u32[]{:S(2)}) copy-start(bf16[256,512]{1,0:T(8,128)(2,1)} %get-tuple-element.28) | copy-start | bytes 786436

commit v2 on v1

v2 whole, which is shorter than its diff:
```python
import functools

import jax
import jax.numpy as jnp
from jax import lax
from jax.experimental import pallas as pl
from jax.experimental.pallas import tpu as pltpu
from jax.sharding import PartitionSpec as P

D = 128
BLK = 128
WIN = 16
CTX = 64
TOK = 256
CHIP = 512
HALF = 2048
NSEG = 16
FACTOR = D ** -0.5
LOG2E = 1.4426950408889634
LOWEST = -1.0e30
F32, BF16, I32 = jnp.float32, jnp.bfloat16, jnp.int32
MESH = pl.DeviceIdType.MESH
NT = (((1,), (1,)), ((), ()))
NN = (((1,), (0,)), ((), ()))
TN = (((0,), (0,)), ((), ()))


def dot(left, right, dims):
    return lax.dot_general(left, right, dims, preferred_element_type=F32)


class Place:
    def __init__(self):
        self.ctx = lax.axis_index("ctx")
        self.kvh = lax.axis_index("kvh")
        self.core = lax.rem(self.ctx, 2)
        self.chip = lax.div(self.ctx, 2)
        self.x = lax.rem(self.chip, 4)

    def sibling(self):
        return (self.ctx + 1 - 2 * self.core, self.kvh)

    def later(self, k):
        x = lax.rem(self.x + k, 4)
        return (self.ctx + 2 * (x - self.x), self.kvh)

    def line(self, step):
        return (lax.rem(self.ctx + CTX + 8 * step, CTX), self.kvh)


def enter(place):
    barrier = pltpu.get_barrier_semaphore()
    peers = [place.sibling(), place.later(1), place.later(2), place.later(3), place.line(1), place.line(-1)]
    for peer in peers:
        pl.semaphore_signal(barrier, inc=1, device_id=peer, device_id_type=MESH)
    pl.semaphore_wait(barrier, len(peers))


def remote(src, dst, send, recv, peer):
    return pltpu.make_async_remote_copy(
        src_ref=src, dst_ref=dst, send_sem=send, recv_sem=recv, device_id=peer, device_id_type=MESH
    )


def fused_kernel(q, k, v, o, lse, do, seg, act,
                 gq, gk, gv,
                 kv, qv, dov, o_v, d_v, rows, theirs, actin, actbuf, firsts,
                 dq_sum, kv_sum, own_sum, parts, far, got, relay, final, dq,
                 load_s, pair_l, pair_s, pair_r, up_s, up_r, line_s, line_r, big_s, big_r, small_s, small_r,
                 back_s, back_r, down_s, down_r, out_s, fin_s, fin_r, q_s, q_r):
    place = Place()
    core, x, chip = place.core, place.x, place.chip
    other = 1 - core
    sib = place.sibling()
    here = pl.ds(pl.multiple_of(core * HALF, HALF), HALF)
    away = pl.ds(pl.multiple_of(other * HALF, HALF), HALF)
    mine = pl.ds(pl.multiple_of(core * TOK, TOK), TOK)
    others = pl.ds(pl.multiple_of(other * TOK, TOK), TOK)

    def part(piece, half):
        source = (k, v)[piece % 2]
        return source.at[:, pl.ds(pl.multiple_of((half * 2 + piece // 2) * D, D), D)]

    def shelf(slot, piece):
        return kv.at[slot, piece]

    local = [pltpu.make_async_copy(part(p, core), kv.at[4, p, mine, :], pair_l.at[p]) for p in range(4)]
    loads = [
        pltpu.make_async_copy(do, d_v, load_s.at[0]),
        pltpu.make_async_copy(o, o_v, load_s.at[1]),
        pltpu.make_async_copy(do.at[:, here], dov.at[mine, :], load_s.at[2]),
        pltpu.make_async_copy(q.at[:, here], qv.at[mine, :], load_s.at[3]),
    ]
    for copy in local + loads:
        copy.start()
    actin[...] = jnp.zeros_like(actin)
    actin[0:2, 0:WIN] = act[...]
    enter(place)

    pair = [remote(part(p, other), kv.at[4, p, mine, :], pair_s.at[p], pair_r.at[p], sib) for p in range(4)]
    big = [remote(do.at[:, away], dov.at[mine, :], big_s.at[0], big_r.at[0], sib),
           remote(q.at[:, away], qv.at[mine, :], big_s.at[1], big_r.at[1], sib)]
    small = [remote(actin, actbuf, small_s.at[0], small_r.at[0], sib),
             remote(theirs, rows.at[core], small_s.at[1], small_r.at[1], sib)]
    for copy in pair + [small[0]] + big:
        copy.start()

    up = [remote(shelf(4, p), shelf(0, p), up_s.at[p], up_r.at[p], place.line(1)) for p in range(4)]
    own_line = [[remote(shelf(4, p), shelf(4 - s, p), line_s.at[s - 1, p], line_r.at[s - 1, p], place.later(s))
                 for p in range(4)] for s in (1, 2, 3)]
    prev_line = [[remote(shelf(0, p), shelf(4 - s, p), line_s.at[s - 1, p], line_r.at[s - 1, p], place.later(s))
                  for p in range(4)] for s in (1, 2, 3)]
    for p in range(4):
        local[p].wait()
        pair[p].wait()
        up[p].start()
        for s in (1, 2, 3):
            @pl.when(x + s < 4)
            def _(s=s, p=p):
                own_line[s - 1][p].start()

    loads[0].wait()
    loads[1].wait()
    spread = jnp.where(lax.broadcasted_iota(I32, (8, 8 * D), 1) // D == lax.broadcasted_iota(I32, (8, 8 * D), 0),
                       1.0, 0.0).astype(BF16)
    for g in range(4):
        cols = slice(g * 8 * D, (g + 1) * 8 * D)
        product = d_v[:, cols].astype(F32) * o_v[:, cols].astype(F32)
        high = product.astype(BF16)
        low = (product - high.astype(F32)).astype(BF16)
        delta = dot(spread, high, NT) + dot(spread, low, NT)
        logs = lse[g * 8:(g + 1) * 8, :] * LOG2E

        @pl.when(core == g // 2)
        def _(delta=delta, logs=logs, g=g):
            rows[core, 0, g % 2] = logs
            rows[core, 1, g % 2] = delta

        @pl.when(core != g // 2)
        def _(delta=delta, logs=logs, g=g):
            theirs[0, g % 2] = logs
            theirs[1, g % 2] = delta

    small[1].start()

    seg_all = seg[...]
    seg_here = seg[pl.ds(chip * 4, 4), :]
    first = jnp.zeros((4, BLK), I32)
    for s in range(1, NSEG):
        first = jnp.where(seg_here == s, jnp.sum((seg_all < s).astype(I32)), first)
    small[0].wait()
    flags = [jnp.where(core == 0, actin[...], actbuf[...]), jnp.where(core == 0, actbuf[...], actin[...])]
    firsts[...] = jnp.full(firsts.shape, 2 ** 30, I32)
    for a in range(4):
        for d in range(WIN):
            flag = jnp.broadcast_to(flags[a // 2][a % 2:a % 2 + 1, d:d + 1], (1, BLK))
            firsts[a, d:d + 1, :] = jnp.where(flag > 0, first[a:a + 1, :], 2 ** 30)
    dq_sum[...] = jnp.zeros_like(dq_sum)

    key_at = lax.broadcasted_iota(I32, (BLK, BLK), 0)
    query_at = lax.broadcasted_iota(I32, (1, BLK), 1)

    def tile(slot, a, h):
        keys = pl.ds(pl.multiple_of(h * 2 * BLK, 2 * BLK), 2 * BLK)
        tokens = pl.ds(pl.multiple_of(a * BLK, BLK), BLK)
        lanes = pl.ds(pl.multiple_of(lax.rem(a, 2) * BLK, BLK), BLK)
        half = lax.div(a, 2)
        bias = []
        for b in range(2):
            rel = slot * 4 + h * 2 + b
            base = (chip * 4 - 16 + rel) * BLK
            low = firsts[a, pl.ds(jnp.maximum(16 + a - rel, 0), 1), :] - base
            high = (chip * 4 + a) * BLK - base + query_at
            bias.append(jnp.where((key_at >= low) & (key_at <= high), 0.0, LOWEST))
        bias = jnp.concatenate(bias, 0)
        for g in range(2):
            key, value = kv[slot, 2 * g, keys, :], kv[slot, 2 * g + 1, keys, :]
            columns = [slice((g * 8 + j) * D, (g * 8 + j + 1) * D) for j in range(8)]
            query = jnp.concatenate([qv[tokens, c] for c in columns], 0)
            cotangent = jnp.concatenate([dov[tokens, c] for c in columns], 0)
            scores = dot(key, query, NT)
            grad_weights = dot(value, cotangent, NT)
            weights, grad_scores = [], []
            for j in range(8):
                lane = slice(j * BLK, (j + 1) * BLK)
                log_row = rows[half, 0, g, j:j + 1, lanes]
                delta_row = rows[half, 1, g, j:j + 1, lanes]
                weight = jnp.exp2(scores[:, lane] * (FACTOR * LOG2E) - log_row + bias)
                weights.append(weight.astype(BF16))
                grad_scores.append((weight * (grad_weights[:, lane] - delta_row)).astype(BF16))
            weights = jnp.concatenate(weights, 1)
            grad_scores = jnp.concatenate(grad_scores, 1)
            kv_sum[2 * g, keys, :] += dot(grad_scores, query, NN)
            kv_sum[2 * g + 1, keys, :] += dot(weights, cotangent, NN)
            dq_sum[a, g] += dot(key, grad_scores, TN)

    def phase(slot, steps, pairs, after=None):
        kv_sum[...] = jnp.zeros_like(kv_sum)

        def step(i, carry):
            for a, h in pairs(i):
                tile(slot, a, h)
            if after is not None:
                after(i)
            return carry

        lax.fori_loop(0, steps, step, 0)

    back = [[remote(parts.at[s - 1, p], got.at[s - 1, p], back_s.at[s - 1, p], back_r.at[s - 1, p], place.later(4 - s))
             for p in range(4)] for s in (1, 2, 3)]

    def full_phase(s):
        for p in range(4):
            prev_line[s - 1][p].wait_recv()
        phase(4 - s, 4, lambda i: [(i, 0), (i, 1)])
        for p in range(4):
            parts[s - 1, p] = (kv_sum[p] * (FACTOR if p % 2 == 0 else 1.0)).astype(BF16)
            back[s - 1][p].start()

    def forward(p):
        remote(shelf(4, p), shelf(0, p), up_s.at[p], up_r.at[p], place.line(1)).wait_recv()
        for s in (1, 3, 2):
            @pl.when(x + s >= 4)
            def _(s=s):
                remote(shelf(0, p), shelf(4 - s, p), line_s.at[s - 1, p], line_r.at[s - 1, p], place.later(s)).start()

    for copy in loads[2:] + big + [small[1]]:
        copy.wait()
    forward(0)
    phase(4, 3, lambda i: [(jnp.where(i == 0, 0, i + 1), 0), (i + 1, jnp.where(i == 0, 0, 1))],
          lambda i: forward(i + 1))
    for p in range(4):
        own_sum[p] = kv_sum[p] * (FACTOR if p % 2 == 0 else 1.0)
    full_phase(1)
    full_phase(3)
    full_phase(2)
    phase(0, 2, lambda i: [(i, i), (2 * i, 1)])
    for p in range(4):
        far[p] = (kv_sum[p] * (FACTOR if p % 2 == 0 else 1.0)).astype(BF16)

    def turn(i, carry):
        a, g = lax.div(i, 2), lax.rem(i, 2)
        tokens = pl.ds(pl.multiple_of(a * BLK, BLK), BLK)
        for j in range(8):
            block = dq_sum[a, g, :, j * BLK:(j + 1) * BLK].T * FACTOR
            dq[tokens, pl.ds(pl.multiple_of((g * 8 + j) * D, D), D)] = block.astype(BF16)
        return carry

    lax.fori_loop(0, 8, turn, 0)
    send_q = remote(dq.at[others, :], gq.at[:, here], q_s.at[0], q_r.at[0], sib)
    send_q.start()
    keep_q = pltpu.make_async_copy(dq.at[mine, :], gq.at[:, here], load_s.at[4])
    keep_q.start()

    down = [remote(relay.at[p], got.at[3, p], down_s.at[p], down_r.at[p], place.line(-1)) for p in range(4)]
    for p in range(4):
        final[...] = far[p].astype(F32)
        for s in (3, 2, 1):
            @pl.when(x + s >= 4)
            def _(s=s, p=p):
                back[s - 1][p].wait_recv()
                final[...] += got[s - 1, p].astype(F32)
        relay[p] = final[...].astype(BF16)
        down[p].start()
    for p in range(4):
        for s in (1, 3, 2):
            @pl.when(x + s < 4)
            def _(s=s, p=p):
                back[s - 1][p].wait_recv()
                own_sum[p] += got[s - 1, p].astype(F32)
    finish, keep = [], []
    for p in range(4):
        down[p].wait_recv()
        far[p] = (own_sum[p] + got[3, p].astype(F32)).astype(BF16)
        target = (gk, gv)[p % 2].at[:, pl.ds(pl.multiple_of((core * 2 + p // 2) * D, D), D)]
        finish.append(remote(far.at[p, others, :], target, fin_s.at[p], fin_r.at[p], sib))
        keep.append(pltpu.make_async_copy(far.at[p, mine, :], target, out_s.at[p]))
        finish[p].start()
        keep[p].start()
    for p in range(4):
        keep[p].wait()
        finish[p].wait()
        up[p].wait_send()
        down[p].wait_send()
        for s in (1, 2, 3):
            prev_line[s - 1][p].wait_send()
            back[s - 1][p].wait_send()
    send_q.wait()
    keep_q.wait()


def body(queries, keys, values, fwd_out, log_sum, out_grad, seg_ids, active):
    anywhere = pl.BlockSpec(memory_space=pl.ANY)
    vmem = pl.BlockSpec(memory_space=pltpu.VMEM)
    dma = pltpu.SemaphoreType.DMA
    seg = seg_ids.reshape(BLK, BLK)
    return tuple(pl.pallas_call(
        fused_kernel,
        out_shape=[
            jax.ShapeDtypeStruct((TOK, 2 * HALF), BF16),
            jax.ShapeDtypeStruct((TOK, 4 * D), BF16),
            jax.ShapeDtypeStruct((TOK, 4 * D), BF16),
        ],
        in_specs=[anywhere, anywhere, anywhere, anywhere, vmem, anywhere, vmem, vmem],
        out_specs=[anywhere] * 3,
        scratch_shapes=[
            pltpu.VMEM((5, 4, CHIP, D), BF16),
            pltpu.VMEM((CHIP, HALF), BF16),
            pltpu.VMEM((CHIP, HALF), BF16),
            pltpu.VMEM((TOK, 2 * HALF), BF16),
            pltpu.VMEM((TOK, 2 * HALF), BF16),
            pltpu.VMEM((2, 2, 2, 8, TOK), F32),
            pltpu.VMEM((2, 2, 8, TOK), F32),
            pltpu.VMEM((8, BLK), I32),
            pltpu.VMEM((8, BLK), I32),
            pltpu.VMEM((4, 24, BLK), I32),
            pltpu.VMEM((4, 2, D, 8 * BLK), F32),
            pltpu.VMEM((4, CHIP, D), F32),
            pltpu.VMEM((4, CHIP, D), F32),
            pltpu.VMEM((3, 4, CHIP, D), BF16),
            pltpu.VMEM((4, CHIP, D), BF16),
            pltpu.VMEM((4, 4, CHIP, D), BF16),
            pltpu.VMEM((4, CHIP, D), BF16),
            pltpu.VMEM((CHIP, D), F32),
            pltpu.VMEM((CHIP, HALF), BF16),
            dma((5,)), dma((4,)), dma((4,)), dma((4,)), dma((4,)), dma((4,)), dma((3, 4)), dma((3, 4)),
            dma((2,)), dma((2,)), dma((2,)), dma((2,)),
            dma((3, 4)), dma((3, 4)), dma((4,)), dma((4,)), dma((4,)), dma((4,)), dma((4,)), dma((1,)), dma((1,)),
        ],
        compiler_params=pltpu.CompilerParams(
            collective_id=0, has_side_effects=True, vmem_limit_bytes=63 * 2 ** 20),
        cost_estimate=pl.CostEstimate(flops=25 * 10 ** 9, bytes_accessed=12 * 2 ** 20, transcendentals=0),
        name="fused",
    )(queries, keys, values, fwd_out, log_sum, out_grad, seg, active))


def solution(mesh):
    placed = (
        P("ctx", "kvh"), P("ctx", "kvh"), P("ctx", "kvh"), P("ctx", "kvh"),
        P("kvh", "ctx"), P("ctx", "kvh"), P(), P("ctx", None),
    )
    return jax.shard_map(
        body, mesh=mesh, in_specs=placed,
        out_specs=(P("ctx", "kvh"), P("ctx", "kvh"), P("ctx", "kvh")),
        check_vma=False,
    )
```

time: 127 us -> 103 us (0.81)
  the two profiles are of different devices: /device:TPU:12 before, /device:TPU:1 now
where the time goes in v2:
time: 103 us
  Pallas kernels  97.8 us (95%)
  local copies, waits for them, and re-layouts  4.6 us (4%)
    pallas_call x1, Pallas kernels, body(): pl.pallas_call(fused_kernel, out_shape=[jax.ShapeDtypeStruct((TOK, 2 * HA...  97.8 us
    unnamed x7, local copies, waits for them, and re-layouts  4.6 us

profile of v2, /device:TPU:1, one launch (start us, length us, event | category | flops | bytes accessed | tf_op | source)
XLA Modules:
  0.0 103.1 jit_solution(14943029806253259811)
XLA Ops:
  0.6 97.8 %fused.1 = (bf16[256,4096]{1,0:T(8,128)(2,1)}, bf16[256,512]{1,0:T(8,128)(2,1)}, bf16[256,512]{1,0:T(8,128)(2,1)}) custom-call(bf16[256,4096]{1,0:T(8,128)(2,1)} %q.1, bf16[256,512]{1,0:T(8,128)(2,1)} %k.1, bf16[256,512]{1,0:T(8,128)(2,1)} %v.1, bf16[256,4096]{1,0:T(8,128)(2,1)} %o.1, f32[32,256]{1,0:T(8,128)} %lse.1, bf16[256,4096]{1,0:T(8,128)(2,1)} %do.1, ...), custom_call_target="tpu_custom_call" | custom-call | flops 24999999488 | bytes 12582912 | tf_op jit(solution)/shard_map/fused/pallas_call | solution.py:297
  98.5 0.0 copy-start.1
  98.5 0.0 copy-start
  98.5 3.2 %copy.14 = bf16[256,4096]{1,0:T(8,128)(2,1)} copy(bf16[256,4096]{1,0:T(8,128)(2,1)} %get-tuple-element.6) | data formatting | bytes 4194304
  101.7 0.0 copy-done.1
  101.7 0.7 copy.15
  102.4 0.0 copy-done
  102.4 0.7 copy.16
Async XLA Ops:
  98.5 3.2 %copy-start.1 = (bf16[256,512]{1,0:T(8,128)(2,1)S(1)}, bf16[256,512]{1,0:T(8,128)(2,1)}, u32[]{:S(2)}) copy-start(bf16[256,512]{1,0:T(8,128)(2,1)} %get-tuple-element.7) | copy-start | bytes 786436
  98.5 3.9 %copy-start = (bf16[256,512]{1,0:T(8,128)(2,1)S(1)}, bf16[256,512]{1,0:T(8,128)(2,1)}, u32[]{:S(2)}) copy-start(bf16[256,512]{1,0:T(8,128)(2,1)} %get-tuple-element.8) | copy-start | bytes 786436

commit v3 on v2

--- a/solution.py
+++ b/solution.py
@@ -114,7 +114,7 @@
         local[p].wait()
         pair[p].wait()
         up[p].start()
-        for s in (1, 2, 3):
+        for s in (1, 3):
             @pl.when(x + s < 4)
             def _(s=s, p=p):
                 own_line[s - 1][p].start()
@@ -160,7 +160,7 @@
     key_at = lax.broadcasted_iota(I32, (BLK, BLK), 0)
     query_at = lax.broadcasted_iota(I32, (1, BLK), 1)
 
-    def tile(slot, a, h):
+    def tile(slot, a, h, heads=(0, 1)):
         keys = pl.ds(pl.multiple_of(h * 2 * BLK, 2 * BLK), 2 * BLK)
         tokens = pl.ds(pl.multiple_of(a * BLK, BLK), BLK)
         lanes = pl.ds(pl.multiple_of(lax.rem(a, 2) * BLK, BLK), BLK)
@@ -173,7 +173,7 @@
             high = (chip * 4 + a) * BLK - base + query_at
             bias.append(jnp.where((key_at >= low) & (key_at <= high), 0.0, LOWEST))
         bias = jnp.concatenate(bias, 0)
-        for g in range(2):
+        for g in heads:
             key, value = kv[slot, 2 * g, keys, :], kv[slot, 2 * g + 1, keys, :]
             columns = [slice((g * 8 + j) * D, (g * 8 + j + 1) * D) for j in range(8)]
             query = jnp.concatenate([qv[tokens, c] for c in columns], 0)
@@ -194,12 +194,13 @@
             kv_sum[2 * g + 1, keys, :] += dot(weights, cotangent, NN)
             dq_sum[a, g] += dot(key, grad_scores, TN)
 
-    def phase(slot, steps, pairs, after=None):
-        kv_sum[...] = jnp.zeros_like(kv_sum)
+    def phase(slot, steps, pairs, after=None, heads=(0, 1)):
+        for g in heads:
+            kv_sum[2 * g:2 * g + 2] = jnp.zeros((2, CHIP, D), F32)
 
         def step(i, carry):
             for a, h in pairs(i):
-                tile(slot, a, h)
+                tile(slot, a, h, heads)
             if after is not None:
                 after(i)
             return carry
@@ -209,9 +210,21 @@
     back = [[remote(parts.at[s - 1, p], got.at[s - 1, p], back_s.at[s - 1, p], back_r.at[s - 1, p], place.later(4 - s))
              for p in range(4)] for s in (1, 2, 3)]
 
+    def send_two():
+        for p in range(4):
+            @pl.when(x < 2)
+            def _(p=p):
+                own_line[1][p].start()
+
+            @pl.when(x >= 2)
+            def _(p=p):
+                prev_line[1][p].start()
+
     def full_phase(s):
         for p in range(4):
             prev_line[s - 1][p].wait_recv()
+        if s == 1:
+            send_two()
         phase(4 - s, 4, lambda i: [(i, 0), (i, 1)])
         for p in range(4):
             parts[s - 1, p] = (kv_sum[p] * (FACTOR if p % 2 == 0 else 1.0)).astype(BF16)
@@ -219,24 +232,65 @@
 
     def forward(p):
         remote(shelf(4, p), shelf(0, p), up_s.at[p], up_r.at[p], place.line(1)).wait_recv()
+        for s in (1, 3):
+            @pl.when(x + s >= 4)
+            def _(s=s):
+                remote(shelf(0, p), shelf(4 - s, p), line_s.at[s - 1, p], line_r.at[s - 1, p], place.later(s)).start()
+
+    def own_pairs(i):
+        i = lax.rem(i + core, 3)
+        return [(jnp.where(i == 0, 0, i + 1), 0), (i + 1, jnp.where(i == 0, 0, 1))]
+
+    def first_step(i):
+        @pl.when(i == 0)
+        def _():
+            forward(0)
+            forward(1)
+            for copy in big + [small[1]]:
+                copy.wait()
+
+        @pl.when(i > 0)
+        def _():
+            forward(i + 1)
+
+    loads[2].wait()
+    loads[3].wait()
+    phase(4, 3, own_pairs, first_step)
+    for p in range(4):
+        own_sum[p] = kv_sum[p] * (FACTOR if p % 2 == 0 else 1.0)
+    def keep_far():
+        for p in range(4):
+            far[p] = (kv_sum[p] * (FACTOR if p % 2 == 0 else 1.0)).astype(BF16)
+
+    phase(0, 2, lambda i: [(i, i), (2 * i, 1)])
+    keep_far()
+    full_phase(1)
+    full_phase(3)
+    for p in range(4):
+        prev_line[1][p].wait_recv()
+    down = [remote(relay.at[p], got.at[3, p], down_s.at[p], down_r.at[p], place.line(-1)) for p in range(4)]
+
+    def pass_down(p):
+        final[...] = far[p].astype(F32)
         for s in (1, 3, 2):
             @pl.when(x + s >= 4)
             def _(s=s):
-                remote(shelf(0, p), shelf(4 - s, p), line_s.at[s - 1, p], line_r.at[s - 1, p], place.later(s)).start()
-
-    for copy in loads[2:] + big + [small[1]]:
-        copy.wait()
-    forward(0)
-    phase(4, 3, lambda i: [(jnp.where(i == 0, 0, i + 1), 0), (i + 1, jnp.where(i == 0, 0, 1))],
-          lambda i: forward(i + 1))
-    for p in range(4):
-        own_sum[p] = kv_sum[p] * (FACTOR if p % 2 == 0 else 1.0)
-    full_phase(1)
-    full_phase(3)
-    full_phase(2)
-    phase(0, 2, lambda i: [(i, i), (2 * i, 1)])
-    for p in range(4):
-        far[p] = (kv_sum[p] * (FACTOR if p % 2 == 0 else 1.0)).astype(BF16)
+                back[s - 1][p].wait_recv()
+                final[...] += got[s - 1, p].astype(F32)
+        relay[p] = final[...].astype(BF16)
+        down[p].start()
+
+    def early(i):
+        @pl.when(i == 0)
+        def _():
+            pass_down(0)
+
+    for g in range(2):
+        phase(2, 2, lambda i: [(2 * i, 0), (2 * i, 1), (2 * i + 1, 0), (2 * i + 1, 1)],
+              early if g == 1 else None, heads=(g,))
+        for p in (2 * g, 2 * g + 1):
+            parts[1, p] = (kv_sum[p] * (FACTOR if p % 2 == 0 else 1.0)).astype(BF16)
+            back[1][p].start()
 
     def turn(i, carry):
         a, g = lax.div(i, 2), lax.rem(i, 2)
@@ -246,22 +300,14 @@
             dq[tokens, pl.ds(pl.multiple_of((g * 8 + j) * D, D), D)] = block.astype(BF16)
         return carry
 
+    pass_down(1)
     lax.fori_loop(0, 8, turn, 0)
     send_q = remote(dq.at[others, :], gq.at[:, here], q_s.at[0], q_r.at[0], sib)
     send_q.start()
     keep_q = pltpu.make_async_copy(dq.at[mine, :], gq.at[:, here], load_s.at[4])
     keep_q.start()
-
-    down = [remote(relay.at[p], got.at[3, p], down_s.at[p], down_r.at[p], place.line(-1)) for p in range(4)]
-    for p in range(4):
-        final[...] = far[p].astype(F32)
-        for s in (3, 2, 1):
-            @pl.when(x + s >= 4)
-            def _(s=s, p=p):
-                back[s - 1][p].wait_recv()
-                final[...] += got[s - 1, p].astype(F32)
-        relay[p] = final[...].astype(BF16)
-        down[p].start()
+    pass_down(2)
+    pass_down(3)
     for p in range(4):
         for s in (1, 3, 2):
             @pl.when(x + s < 4)

time: 103 us -> 87.9 us (0.85)
  Pallas kernels: 97.8 us -> 82.4 us
    pallas_call x1, Pallas kernels: 97.8 us -> 82.4 us  [body(): pl.pallas_call(fused_kernel, out_shape=[jax.ShapeDtypeStruct((TOK, 2 * HA...]
where the time goes in v3:
time: 87.9 us; the launch traced here: 87.7 us
  Pallas kernels  82.4 us (94%)
  local copies, waits for them, and re-layouts  4.6 us (5%)
    pallas_call x1, Pallas kernels, body(): pl.pallas_call(fused_kernel, out_shape=[jax.ShapeDtypeStruct((TOK, 2 * HA...  82.4 us
    unnamed x7, local copies, waits for them, and re-layouts  4.6 us

profile of v3, /device:TPU:1, one launch (start us, length us, event | category | flops | bytes accessed | tf_op | source)
XLA Modules:
  0.0 87.7 jit_solution(16275252508061123486)
XLA Ops:
  0.6 82.4 %fused.1 = (bf16[256,4096]{1,0:T(8,128)(2,1)}, bf16[256,512]{1,0:T(8,128)(2,1)}, bf16[256,512]{1,0:T(8,128)(2,1)}) custom-call(bf16[256,4096]{1,0:T(8,128)(2,1)} %q.1, bf16[256,512]{1,0:T(8,128)(2,1)} %k.1, bf16[256,512]{1,0:T(8,128)(2,1)} %v.1, bf16[256,4096]{1,0:T(8,128)(2,1)} %o.1, f32[32,256]{1,0:T(8,128)} %lse.1, bf16[256,4096]{1,0:T(8,128)(2,1)} %do.1, ...), custom_call_target="tpu_custom_call" | custom-call | flops 24999999488 | bytes 12582912 | tf_op jit(solution)/shard_map/fused/pallas_call | solution.py:343
  83.1 0.0 copy-start.1
  83.1 0.0 copy-start
  83.1 3.2 %copy.14 = bf16[256,4096]{1,0:T(8,128)(2,1)} copy(bf16[256,4096]{1,0:T(8,128)(2,1)} %get-tuple-element.6) | data formatting | bytes 4194304
  86.3 0.0 copy-done.1
  86.3 0.7 copy.15
  87.0 0.0 copy-done
  87.0 0.7 copy.16
Async XLA Ops:
  83.1 3.2 %copy-start.1 = (bf16[256,512]{1,0:T(8,128)(2,1)S(1)}, bf16[256,512]{1,0:T(8,128)(2,1)}, u32[]{:S(2)}) copy-start(bf16[256,512]{1,0:T(8,128)(2,1)} %get-tuple-element.7) | copy-start | bytes 786436
  83.1 3.9 %copy-start = (bf16[256,512]{1,0:T(8,128)(2,1)S(1)}, bf16[256,512]{1,0:T(8,128)(2,1)}, u32[]{:S(2)}) copy-start(bf16[256,512]{1,0:T(8,128)(2,1)} %get-tuple-element.8) | copy-start | bytes 786436
